TPU v7x, 512 devices: a whole 4x8x8 slice. The times are simulated.
512 devices in a mesh: face: 8 (over y), row: 8 (over z_hi, core), col: 8 (over z_lo, x).
Axes of the slice: x: 4, y: 8, z: 8 (z_hi: 4, z_lo: 2; z = z_hi * 2 + z_lo), core: 2. Of those that a mesh axis runs over, the one named last changes fastest.
Arguments:
- block_in: bfloat16 [8, 64, 64, 1024], P('face', None, 'row', 'col'), may hold values from -6 to 6
- hidden_state: bfloat16 [8, 64, 64, 1024], P('face', None, 'row', 'col'), may hold values from -0.8984375 to 0.8984375
- state_cotangent: bfloat16 [8, 64, 64, 1024], P('face', None, 'row', 'col'), may hold values from -6 to 6
- kernel: float32 [64, 49], replicated, may hold values from -0.875 to 0.875
- expand_weight: bfloat16 [64, 256], replicated, may hold values from -0.75 to 0.75
- reduce_weight: bfloat16 [256, 64], replicated, may hold values from -0.375 to 0.375
- gates_weight: bfloat16 [128, 128], replicated, may hold values from -0.5 to 0.5
- candidate_weight: bfloat16 [128, 64], replicated, may hold values from -0.5 to 0.5
- seam_face: int32 [8, 4], replicated, may hold values from 0 to 7, as said below
- seam_code: int32 [8, 4], replicated, may hold values from 0 to 3, as said below
Outputs:
- next_state: bfloat16 [8, 64, 64, 1024], P('face', None, 'row', 'col')
- grad_input: bfloat16 [8, 64, 64, 1024], P('face', None, 'row', 'col')
- grad_state: bfloat16 [8, 64, 64, 1024], P('face', None, 'row', 'col')
- grad_kernel: float32 [64, 49], replicated
- grad_expand: float32 [64, 256], replicated
- grad_reduce: float32 [256, 64], replicated
- grad_gates: float32 [128, 128], replicated
- grad_candidate: float32 [128, 64], replicated
Inputs may be any that keep to these rules, and one draw needn't show every extreme that they name: `seam_face`: column s holds, for every face, the partner face across its seam s (0 north, 1 south, 2 west, 3 east); each column is a permutation of the 8 faces. `seam_code`: bit 0 set: the partner's edge is on the same side as this one (a half turn), else on the opposite side; bit 1 set: the seam runs in reverse order along the edge. Each of the four codes appears 8 times.
All inputs are finite; a program needn't handle non-finite values.
Results may differ from a plain program's by a relative error of at most 0.019.
Values may be sent and summed in bfloat16 or wider, within the bound.
A program may use at most 64 MiB of HBM per device.

v0:
```python
import math

import jax
import jax.numpy as jnp
from jax import lax
from jax.sharding import PartitionSpec as P

KSIDE = 7
RIM = 3


def swapped(block, axis, distance):
    count = lax.axis_size(axis)
    route = []
    for low in range(count):
        high = low | 1 << distance
        if high != low and high < count:
            route += [(low, high), (high, low)]
    return lax.ppermute(block, axis, route)


def padded_2(block, sides, width):
    for axis, dim in sides:
        count = lax.axis_size(axis)
        forward = [(i, i + 1) for i in range(count - 1)]
        forward.append((count - 1, 0))
        backward = [(target, source) for source, target in forward]
        low = lax.ppermute(
            lax.slice_in_dim(block, block.shape[dim] - width, None, axis=dim), axis, forward
        )
        high = lax.ppermute(lax.slice_in_dim(block, 0, width, axis=dim), axis, backward)
        block = jnp.concatenate([low, block, high], axis=dim)
    return block


def contract(weight, values):
    return jnp.dot(weight.astype(jnp.bfloat16).T, values, preferred_element_type=jnp.float32)


def block_step(
    padded,
    center,
    prior_state,
    kernel,
    expand_weight,
    reduce_weight,
    gates_weight,
    candidate_weight,
):
    channels, height, tile_width = center.shape
    cell_count = height * tile_width
    source = padded.astype(jnp.float32)
    summed = jnp.zeros((channels, height, tile_width), jnp.float32)
    for offset in range(KSIDE * KSIDE):
        shift_row = offset // KSIDE
        shift_col = offset % KSIDE
        summed = (
            summed
            + kernel[:, offset][:, None, None]
            * source[:, shift_row : shift_row + height, shift_col : shift_col + tile_width]
        )
    flattened = summed.reshape(channels, cell_count)
    average = jnp.mean(flattened, axis=0)
    centered = flattened - average
    variance = jnp.mean(centered * centered, axis=0)
    normed = (centered * lax.rsqrt(variance + 1e-06)).astype(jnp.bfloat16)
    hidden = contract(expand_weight, normed)
    activated = jax.nn.gelu(hidden, approximate=False).astype(jnp.bfloat16)
    mixed_out = contract(reduce_weight, activated)
    output = (center.reshape(channels, cell_count).astype(jnp.float32) + mixed_out).astype(
        jnp.bfloat16
    )
    previous = prior_state.reshape(channels, cell_count)
    previous_float = previous.astype(jnp.float32)
    gate_values = jax.nn.sigmoid(
        contract(gates_weight, jnp.concatenate([output, previous], axis=0))
    )
    update = gate_values[:channels]
    reset_gate = gate_values[channels:]
    reset_state = (reset_gate * previous_float).astype(jnp.bfloat16)
    proposal = jnp.tanh(contract(candidate_weight, jnp.concatenate([output, reset_state], axis=0)))
    result = ((1.0 - update) * previous_float + update * proposal).astype(jnp.bfloat16)
    return result.reshape(channels, height, tile_width)


def orient(edge_strip, same_side, reverse_flag, depth_axis, length_axis):
    turned = jnp.where(same_side, jnp.flip(edge_strip, depth_axis), edge_strip)
    return jnp.where(reverse_flag, jnp.flip(turned, length_axis), turned)


def table_entry(lookup, face_index, side_number):
    chosen = (jnp.arange(lookup.shape[0])[:, None] == face_index) & (
        jnp.arange(4)[None, :] == side_number
    )
    return jnp.sum(jnp.where(chosen, lookup, 0))


def table_column(lookup, side_number):
    return jnp.sum(jnp.where(jnp.arange(4)[None, :] == side_number, lookup, 0), axis=1)


def seam_plan(seam_face, seam_code, face_index, side_number):
    partner = table_entry(seam_face, face_index, side_number)
    code_value = table_entry(seam_code, face_index, side_number)
    same_side = code_value % 2 == 1
    reverse_flag = code_value // 2 == 1
    lower_side = side_number % 2 == 0
    kind_index = jnp.where(lower_side, 1 - code_value % 2, code_value % 2)
    partners = table_column(seam_face, side_number)
    codes_all = table_column(seam_code, side_number)
    senders = (
        (partners == face_index)[:, None] & (codes_all[:, None] == jnp.arange(4)[None, :])
    ).astype(jnp.float32)
    return (partner, same_side, reverse_flag, kind_index, lower_side, senders)


def slot_weights(reverse_flag, kind_index):
    rows_hot = jnp.arange(2)[:, None] == reverse_flag.astype(jnp.int32)
    kinds_hot = jnp.arange(2)[None, :] == kind_index
    return (rows_hot & kinds_hot).astype(jnp.float32)


def partner_folder(seam_setup, pieces):
    labels = jnp.arange(pieces.shape[0])
    face_hot = (labels == seam_setup[0]).astype(jnp.float32)
    return jnp.tensordot(face_hot, pieces.astype(jnp.float32), axes=1)


def gathered_strip(gathered, seam_setup, depth_axis, length_axis):
    chosen = jnp.tensordot(slot_weights(seam_setup[2], seam_setup[3]), gathered, axes=2)
    return orient(chosen, seam_setup[1], seam_setup[2], depth_axis, length_axis).astype(
        jnp.bfloat16
    )


def returned_terms(seam_grad, seam_setup, depth_axis, length_axis, face_total):
    oriented = orient(seam_grad, seam_setup[1], seam_setup[2], depth_axis, length_axis)
    face_hot = (jnp.arange(face_total) == seam_setup[0]).astype(jnp.float32)
    return jnp.einsum(
        "f,mk,cab->fmkcab", face_hot, slot_weights(seam_setup[2], seam_setup[3]), oriented
    )


def mirror_columns(values):
    for bit_number in range(lax.axis_size("col").bit_length() - 1):
        values = swapped(values, "col", bit_number)
    return values


def mirror_rows(values):
    for bit_number in range(lax.axis_size("row").bit_length() - 1):
        values = swapped(values, "row", bit_number)
    return values


def mirror_columns_back(values):
    for bit_number in range(lax.axis_size("col").bit_length() - 1):
        values = swapped(values.astype(jnp.bfloat16), "col", bit_number).astype(values.dtype)
    return values


def mirror_rows_back(values):
    for bit_number in range(lax.axis_size("row").bit_length() - 1):
        values = swapped(values, "row", bit_number)
    return values


def seam_rows_forward(stacked, seam_setup):
    gathered = partner_folder(seam_setup, lax.all_gather(stacked[None], "face", axis=0, tiled=True))
    return gathered_strip(gathered, seam_setup, 1, 2)


def seam_columns_forward(stacked, seam_setup):
    gathered = partner_folder(seam_setup, lax.all_gather(stacked[None], "face", axis=0, tiled=True))
    return gathered_strip(gathered, seam_setup, 2, 1)


def seam_rows_backward(seam_grad, seam_setup, face_total):
    terms = returned_terms(seam_grad, seam_setup, 1, 2, face_total)
    return lax.psum_scatter(
        terms.astype(jnp.bfloat16), "face", scatter_dimension=0, tiled=True
    ).astype(jnp.float32)[0]


def seam_columns_backward(seam_grad, seam_setup, face_total):
    terms = returned_terms(seam_grad, seam_setup, 2, 1, face_total)
    return lax.psum_scatter(
        terms.astype(jnp.bfloat16), "face", scatter_dimension=0, tiled=True
    ).astype(jnp.float32)[0]


def body(
    block_in,
    hidden_state,
    state_cotangent,
    kernel,
    expand_weight,
    reduce_weight,
    gates_weight,
    candidate_weight,
    seam_face,
    seam_code,
):
    center = block_in[0]
    prior_state = hidden_state[0]
    cotangent = state_cotangent[0]
    face_total = seam_face.shape[0]
    face_index = lax.axis_index("face")
    row_index = lax.axis_index("row")
    column_index = lax.axis_index("col")
    at_top = row_index == 0
    at_bottom = row_index == lax.axis_size("row") - 1
    at_left = column_index == 0
    at_right = column_index == lax.axis_size("col") - 1
    extended = padded_2(center, (("row", 1),), RIM)
    above_rows = extended[:, :RIM]
    below_rows = extended[:, -RIM:]
    top_strip = jnp.where(at_top, center[:, :RIM], below_rows)
    bottom_strip = jnp.where(at_top, above_rows, center[:, -RIM:])
    row_pair = jnp.stack([top_strip, bottom_strip])
    row_stack = jnp.stack([row_pair, mirror_columns(row_pair)])
    row_setup = seam_plan(seam_face, seam_code, face_index, jnp.where(at_top, 0, 1))
    row_seam = seam_rows_forward(row_stack, row_setup)
    padded_rows = jnp.concatenate(
        [
            jnp.where(at_top, row_seam, above_rows),
            center,
            jnp.where(at_bottom, row_seam, below_rows),
        ],
        axis=1,
    )
    widened = padded_2(padded_rows, (("col", 2),), RIM)
    west_side = widened[:, :, :RIM]
    east_side = widened[:, :, -RIM:]
    left_strip = jnp.where(at_left, padded_rows[:, :, :RIM], east_side)
    right_strip = jnp.where(at_left, west_side, padded_rows[:, :, -RIM:])
    column_pair = jnp.stack([left_strip, right_strip])
    column_stack = jnp.stack([column_pair, mirror_rows(column_pair)])
    column_setup = seam_plan(seam_face, seam_code, face_index, jnp.where(at_left, 2, 3))
    column_seam = seam_columns_forward(column_stack, column_setup)
    padded = jnp.concatenate(
        [
            jnp.where(at_left, column_seam, west_side),
            padded_rows,
            jnp.where(at_right, column_seam, east_side),
        ],
        axis=2,
    )
    next_tile, pullback = jax.vjp(
        block_step,
        padded,
        center,
        prior_state,
        kernel,
        expand_weight.astype(jnp.float32),
        reduce_weight.astype(jnp.float32),
        gates_weight.astype(jnp.float32),
        candidate_weight.astype(jnp.float32),
    )
    (
        padded_grad,
        center_grad,
        prior_grad,
        kernel_grad,
        expand_grad,
        reduce_grad,
        gates_grad,
        candidate_grad,
    ) = pullback(cotangent)
    padded_float = padded_grad.astype(jnp.float32)
    west_grad = padded_float[:, :, :RIM]
    east_grad = padded_float[:, :, -RIM:]
    rows_grad = padded_float[:, :, RIM:-RIM]
    column_seam_grad = jnp.where(at_left, west_grad, jnp.where(at_right, east_grad, 0.0))
    west_back = jnp.where(at_left, 0.0, west_grad)
    east_back = jnp.where(at_right, 0.0, east_grad)
    column_collected = seam_columns_backward(column_seam_grad, column_setup, face_total)
    column_pair_grad = column_collected[0] + mirror_rows_back(column_collected[1])
    rows_grad = rows_grad.at[:, :, :RIM].add(jnp.where(at_left, column_pair_grad[0], 0.0))
    rows_grad = rows_grad.at[:, :, -RIM:].add(jnp.where(at_left, 0.0, column_pair_grad[1]))
    east_back = east_back + jnp.where(at_left, 0.0, column_pair_grad[0])
    west_back = west_back + jnp.where(at_left, column_pair_grad[1], 0.0)
    column_return = padded_2(jnp.concatenate([west_back, east_back], axis=2), (("col", 2),), RIM)
    rows_grad = rows_grad.at[:, :, :RIM].add(column_return[:, :, :RIM])
    rows_grad = rows_grad.at[:, :, -RIM:].add(column_return[:, :, -RIM:])
    north_grad = rows_grad[:, :RIM]
    south_grad = rows_grad[:, -RIM:]
    input_grad = rows_grad[:, RIM:-RIM] + center_grad.astype(jnp.float32)
    row_seam_grad = jnp.where(at_top, north_grad, jnp.where(at_bottom, south_grad, 0.0))
    north_back = jnp.where(at_top, 0.0, north_grad)
    south_back = jnp.where(at_bottom, 0.0, south_grad)
    row_collected = seam_rows_backward(row_seam_grad, row_setup, face_total)
    row_pair_grad = row_collected[0] + mirror_columns_back(row_collected[1])
    input_grad = input_grad.at[:, :RIM].add(jnp.where(at_top, row_pair_grad[0], 0.0))
    input_grad = input_grad.at[:, -RIM:].add(jnp.where(at_top, 0.0, row_pair_grad[1]))
    south_back = south_back + jnp.where(at_top, 0.0, row_pair_grad[0])
    north_back = north_back + jnp.where(at_top, row_pair_grad[1], 0.0)
    row_return = padded_2(
        jnp.concatenate([north_back, south_back], axis=1).astype(jnp.bfloat16), (("row", 1),), RIM
    ).astype(jnp.float32)
    input_grad = input_grad.at[:, :RIM].add(row_return[:, :RIM])
    input_grad = input_grad.at[:, -RIM:].add(row_return[:, -RIM:])
    summed_grads = lax.psum(
        (kernel_grad, expand_grad, reduce_grad, gates_grad, candidate_grad), ("face", "row", "col")
    )
    cell_total = (
        lax.axis_size("face")
        * lax.axis_size("row")
        * lax.axis_size("col")
        * center.shape[1]
        * center.shape[2]
    )
    grad_scale = 1.0 / math.sqrt(cell_total)
    return (
        next_tile[None],
        input_grad.astype(jnp.bfloat16)[None],
        prior_grad[None],
        summed_grads[0] * grad_scale,
        summed_grads[1] * grad_scale,
        summed_grads[2] * grad_scale,
        summed_grads[3] * grad_scale,
        summed_grads[4] * grad_scale,
    )


def solution(mesh):
    return jax.shard_map(
        body,
        mesh=mesh,
        in_specs=(
            P("face", None, "row", "col"),
            P("face", None, "row", "col"),
            P("face", None, "row", "col"),
            P(),
            P(),
            P(),
            P(),
            P(),
            P(),
            P(),
        ),
        out_specs=(
            P("face", None, "row", "col"),
            P("face", None, "row", "col"),
            P("face", None, "row", "col"),
            P(),
            P(),
            P(),
            P(),
            P(),
        ),
        check_vma=False,
    )
```

profile of v0, /device:TPU:1, one launch (start us, length us, event | category | flops | bytes accessed | tf_op | source)
XLA Modules:
  0.0 749.7 jit_solution(17612550971865298028)
XLA Ops:
  8.2 8.8 %collective-permute-start = (bf16[64,3,128]{2,0,1:T(8,128)(2,1)S(1)}, bf16[64,3,128]{2,0,1:T(8,128)(2,1)S(1)}, u32[]{:S(2)}, u32[]{:S(2)}) collective-permute-start(bf16[64,3,128]{2,0,1:T(8,128)(2,1)S(1)} %slice.703), channel_id=1, source_target_pairs={{8,0},{16,8},{24,16},{32,24},{40,32},{48,40},{56,48},{0,56},{9,1},... | collective-permute-start | bytes 147464 | tf_op jit(solution)/shard_map/ppermute | solution.py:31
  17.8 1.9 collective-permute-start.1
  19.8 4.7 collective-permute-done.1
  24.5 3.1 collective-permute-start.2
  27.6 2.2 collective-permute-done.2
  29.8 4.6 collective-permute-start.3
  34.5 2.5 collective-permute-done.3
  37.0 2.8 collective-permute-start.4
  39.8 2.6 collective-permute-done.4
  43.2 1.4 fusion.126
  50.9 36.8 %all-gather.4.cloned.1.call-done = bf16[16,2,64,3,128]{4,2,3,1,0:T(8,128)(2,1)} async-done(((bf16[2,2,64,3,128]{4,2,3,1,0:T(8,128)(2,1)}), bf16[16,2,64,3,128]{4,2,3,1,0:T(8,128)(2,1)}) %all-gather.4.cloned.1.call-update) | async-done | bytes 1572880 | tf_op jit(solution)/shard_map/all_gather | solution.py:169
  87.7 3.1 fusion.2
  91.7 5.4 collective-permute-start.5
  97.1 2.9 collective-permute-done.5
  100.2 1.9 collective-permute-start.6
  102.4 7.1 collective-permute-done.6
  110.0 8.7 %collective-permute-start.7 = (bf16[2,64,14,3]{1,0,3,2:T(2,128)(2,1)S(1)}, bf16[2,64,14,3]{1,0,3,2:T(2,128)(2,1)S(1)}, u32[]{:S(2)}, u32[]{:S(2)}) collective-permute-start(bf16[2,64,14,3]{1,0,3,2:T(2,128)(2,1)S(1)} %pad_maximum_fusion.13), channel_id=1, source_target_pairs={{0,8},{8,0},{16,24},{24,16},{32,40},{40,32},{48,56},{56,48},{1,9},... | collective-permute-start | bytes 32264 | tf_op jit(solution)/shard_map/ppermute | solution.py:19
  118.7 1.8 compare_convert_fusion
  120.5 4.3 collective-permute-start.8
  125.0 1.6 collective-permute-done.8
  126.6 6.1 collective-permute-start.9
  132.8 2.3 collective-permute-done.9
  135.1 19.1 %all-gather.1 = bf16[16,2,64,14,3]{2,1,4,3,0:T(2,128)(2,1)S(1)} all-gather(bf16[2,2,64,14,3]{2,1,4,3,0:T(2,128)(2,1)S(1)} %pad_maximum_fusion.12), channel_id=3, replica_groups=mesh['face'=8,'row'=8,'col'=8] {'face'}, dimensions={0}, use_global_device_ids=true | all-gather | bytes 193536 | tf_op jit(solution)/shard_map/all_gather | solution.py:174
  156.2 3.8 fusion.150
  160.0 3.0 fusion.23
  168.4 1.8 fusion.93
  171.9 7.0 fusion.44
  180.1 1.2 broadcast_select_fusion.1
  181.3 4.9 fusion
  186.3 91.5 %reduce-scatter.3.cloned.1.call-done = bf16[1,2,2,64,14,3]{5,3,4,2,1,0:T(8,128)(2,1)} async-done(((bf16[8,2,2,64,14,3]{5,3,4,2,1,0:T(8,128)(2,1)}), bf16[1,2,2,64,14,3]{5,3,4,2,1,0:T(8,128)(2,1)}) %reduce-scatter.3.cloned.1.call-update) | async-done | bytes 21520 | tf_op jit(solution)/shard_map/reduce_scatter | solution.py:187
  277.8 1.4 convert_element_type.209
  279.2 1.2 copy-done.1
  281.4 1.5 copy.177
  282.9 2.5 collective-permute-start.10
  286.3 4.5 collective-permute-start.11
  290.9 1.4 collective-permute-done.11
  292.3 9.0 %collective-permute-start.12 = (f32[2,64,14,3]{1,0,3,2:T(2,128)S(1)}, f32[2,64,14,3]{1,0,3,2:T(2,128)S(1)}, u32[]{:S(2)}, u32[]{:S(2)}) collective-permute-start(f32[2,64,14,3]{1,0,3,2:T(2,128)S(1)} %collective-permute-done.11), channel_id=1, source_target_pairs={{0,32},{32,0},{8,40},{40,8},{16,48},{48,16},{24,56},{56,24},{1,33}... | collective-permute-start | bytes 64520 | tf_op jit(solution)/shard_map/ppermute | solution.py:19
  302.7 1.3 copy.178
  304.0 1.6 fusion.41
  305.6 1.5 bitcast_add_fusion
  307.1 3.2 collective-permute-start.13
  310.3 4.1 scatter-add.26
  314.4 1.2 slice_add_fusion.2
  315.6 4.3 collective-permute-start.14
  319.9 6.3 scatter-add.29
  327.3 4.1 scatter-add.30
  332.6 6.3 scatter-add.31
  339.7 1.6 fusion.1
  343.6 1.5 fusion.75
  345.2 1.5 fusion.57
  347.2 99.0 %all-reduce.100 = (f32[64,49]{0,1:T(8,128)S(1)}, f32[128,64]{0,1:T(8,128)S(1)}) all-reduce(f32[64,49]{0,1:T(8,128)S(1)} %pad_add_fusion, f32[128,64]{0,1:T(8,128)S(1)} %fusion.20), channel_id=1, replica_groups=mesh['face'=8,'row'=8,'col'=8] {'face','row','col'}, use_global_device_ids=true, to_apply=%region_59.60 | all-reduce | flops 11328 | bytes 90624 | tf_op jit(solution)/shard_map/psum | solution.py:303
  447.5 1.9 fusion.18
  450.2 1.9 fusion.19
  453.0 3.7 collective-permute-start.15
  456.7 258.2 %all-reduce.104.cloned.1.call-done = (f32[64,256]{1,0:T(8,128)}, f32[256,64]{0,1:T(8,128)}, f32[128,128]{1,0:T(8,128)}) async-done(((f32[64,256]{1,0:T(8,128)}, f32[256,64]{0,1:T(8,128)}, f32[128,128]{1,0:T(8,128)}), (f32[64,256]{1,0:T(8,128)}, f32[256,64]{0,1:T(8,128)}, f32[128,128]{1,0:T(8,128)})) %all-reduce.104.cloned.1.call-update) | async-done | bytes 196624 | tf_op jit(solution)/shard_map/psum | solution.py:303
  714.9 1.5 broadcast_multiply_fusion.2
  716.4 4.3 collective-permute-start.16
  720.8 1.5 broadcast_multiply_fusion.1
  722.2 2.4 collective-permute-done.16
  724.6 1.9 collective-permute-start.17
  726.6 3.9 collective-permute-done.17
  731.5 4.0 collective-permute-start.18
  735.4 1.9 collective-permute-start.19
  738.0 4.3 collective-permute-done.19
  (194 shorter events, 30.2 us)
Async XLA Ops:
  7.2 152.8 %copy-start = (bf16[64,256]{1,0:T(8,128)(2,1)S(1)}, bf16[64,256]{1,0:T(8,128)(2,1)}, u32[]{:S(2)}) copy-start(bf16[64,256]{1,0:T(8,128)(2,1)} %param.30) | copy-start | bytes 98308
  7.2 43.7 %copy-start.34 = (f32[64,49]{0,1:T(8,128)S(1)}, f32[64,49]{0,1:T(8,128)}, u32[]{:S(2)}) copy-start(f32[64,49]{0,1:T(8,128)} %param.29) | copy-start | bytes 37636
  7.2 80.5 %all-gather.4.cloned.1.call-start = ((), (), s32[]{:S(2)}) async-start(), calls=%async_computation.4 | async-start | bytes 1769472 | tf_op jit(solution)/shard_map/all_gather | solution.py:169
  8.2 9.7 %collective-permute-start = (bf16[64,3,128]{2,0,1:T(8,128)(2,1)S(1)}, bf16[64,3,128]{2,0,1:T(8,128)(2,1)S(1)}, u32[]{:S(2)}, u32[]{:S(2)}) collective-permute-start(bf16[64,3,128]{2,0,1:T(8,128)(2,1)S(1)} %slice.703), channel_id=1, source_target_pairs={{8,0},{16,8},{24,16},{32,24},{40,32},{48,40},{56,48},{0,56},{9,1},... | collective-permute-start | bytes 147464 | tf_op jit(solution)/shard_map/ppermute | solution.py:31
  17.8 6.6 collective-permute-start.1
  24.5 5.4 collective-permute-start.2
  29.8 7.2 collective-permute-start.3
  37.0 5.3 collective-permute-start.4
  43.1 234.7 %reduce-scatter.3.cloned.1.call-start = ((), (), s32[]{:S(2)}) async-start(), calls=%async_computation.2 | async-start | bytes 8257536 | tf_op jit(solution)/shard_map/reduce_scatter | solution.py:187
  91.4 33.5 %copy-start.23 = (bf16[1,64,8,128]{3,2,1,0:T(8,128)(2,1)S(1)}, bf16[1,64,8,128]{3,2,1,0:T(8,128)(2,1)}, u32[]{:S(2)}) copy-start(bf16[1,64,8,128]{3,2,1,0:T(8,128)(2,1)} %param.27) | copy-start | bytes 393220
  91.5 33.5 %copy-start.29 = (bf16[1,64,8,128]{3,2,1,0:T(8,128)(2,1)S(1)}, bf16[1,64,8,128]{3,2,1,0:T(8,128)(2,1)}, u32[]{:S(2)}) copy-start(bf16[1,64,8,128]{3,2,1,0:T(8,128)(2,1)} %param.28) | copy-start | bytes 393220
  91.6 33.4 %copy-start.25 = (bf16[1,64,8,128]{3,2,1,0:T(8,128)(2,1)S(1)}, bf16[1,64,8,128]{3,2,1,0:T(8,128)(2,1)}, u32[]{:S(2)}) copy-start(bf16[1,64,8,128]{3,2,1,0:T(8,128)(2,1)} %param.26) | copy-start | bytes 393220
  91.7 8.4 %collective-permute-start.5 = (bf16[64,14,3]{2,0,1:T(8,128)(2,1)S(1)}, bf16[64,14,3]{2,0,1:T(8,128)(2,1)S(1)}, u32[]{:S(2)}, u32[]{:S(2)}) collective-permute-start(bf16[64,14,3]{2,0,1:T(8,128)(2,1)S(1)} %bitcast.654), channel_id=1, source_target_pairs={{1,0},{2,1},{3,2},{4,3},{5,4},{6,5},{7,6},{0,7},{9,8},{10,9},{11,1... | collective-permute-start | bytes 16136 | tf_op jit(solution)/shard_map/ppermute | solution.py:31
  100.2 9.3 %collective-permute-start.6 = (bf16[64,14,3]{2,0,1:T(8,128)(2,1)S(1)}, bf16[64,14,3]{2,0,1:T(8,128)(2,1)S(1)}, u32[]{:S(2)}, u32[]{:S(2)}) collective-permute-start(bf16[64,14,3]{2,0,1:T(8,128)(2,1)S(1)} %get-tuple-element.247), channel_id=1, source_target_pairs={{0,1},{1,2},{2,3},{3,4},{4,5},{5,6},{6,7},{7,0},{8,9},{9,10},{10,1... | collective-permute-start | bytes 16136 | tf_op jit(solution)/shard_map/ppermute | solution.py:28
  110.0 10.5 %collective-permute-start.7 = (bf16[2,64,14,3]{1,0,3,2:T(2,128)(2,1)S(1)}, bf16[2,64,14,3]{1,0,3,2:T(2,128)(2,1)S(1)}, u32[]{:S(2)}, u32[]{:S(2)}) collective-permute-start(bf16[2,64,14,3]{1,0,3,2:T(2,128)(2,1)S(1)} %pad_maximum_fusion.13), channel_id=1, source_target_pairs={{0,8},{8,0},{16,24},{24,16},{32,40},{40,32},{48,56},{56,48},{1,9},... | collective-permute-start | bytes 32264 | tf_op jit(solution)/shard_map/ppermute | solution.py:19
  120.5 6.2 collective-permute-start.8
  124.9 39.0 %copy-start.26 = (bf16[8,8,8,128]{3,1,2,0:T(8,128)(2,1)}, bf16[8,8,8,128]{3,1,2,0:T(8,128)(2,1)S(1)}, u32[]{:S(2)}) copy-start(bf16[8,8,8,128]{3,1,2,0:T(8,128)(2,1)S(1)} %copy.406) | copy-start | bytes 393220
  125.0 40.7 %copy-start.2 = (f32[8,8,8,128]{3,2,1,0:T(8,128)}, f32[8,8,8,128]{3,2,1,0:T(8,128)S(1)}, u32[]{:S(2)}) copy-start(f32[8,8,8,128]{3,2,1,0:T(8,128)S(1)} %convert.33) | copy-start | bytes 786436
  126.6 8.4 %collective-permute-start.9 = (bf16[2,64,14,3]{1,0,3,2:T(2,128)(2,1)S(1)}, bf16[2,64,14,3]{1,0,3,2:T(2,128)(2,1)S(1)}, u32[]{:S(2)}, u32[]{:S(2)}) collective-permute-start(bf16[2,64,14,3]{1,0,3,2:T(2,128)(2,1)S(1)} %collective-permute-done.8), channel_id=1, source_target_pairs={{0,32},{32,0},{8,40},{40,8},{16,48},{48,16},{24,56},{56,24},{1,33}... | collective-permute-start | bytes 32264 | tf_op jit(solution)/shard_map/ppermute | solution.py:19
  160.0 3.0 copy-start.33
  160.0 3.9 copy-start.32
  163.1 2.1 copy-start.30
  165.4 1.3 copy-start.5
  165.7 1.7 copy-start.11
  166.5 0.9 copy-start.7
  166.5 0.9 copy-start.9
  167.4 0.9 copy-start.15
  186.3 265.8 %reduce-scatter.5.cloned.1.call-start = ((), (), s32[]{:S(2)}) async-start(), calls=%async_computation.3 | async-start | bytes 1769472 | tf_op jit(solution)/shard_map/reduce_scatter | solution.py:180
  279.2 1.3 copy-start.1
  280.4 20.9 %copy-start.43 = (f32[8]{0:T(128)S(1)}, f32[8]{0:T(128)}, u32[]{:S(2)}) copy-start(f32[8]{0:T(128)} %get-tuple-element.312) | copy-start | bytes 100
  282.9 3.4 collective-permute-start.10
  286.3 6.0 collective-permute-start.11
  292.3 10.4 %collective-permute-start.12 = (f32[2,64,14,3]{1,0,3,2:T(2,128)S(1)}, f32[2,64,14,3]{1,0,3,2:T(2,128)S(1)}, u32[]{:S(2)}, u32[]{:S(2)}) collective-permute-start(f32[2,64,14,3]{1,0,3,2:T(2,128)S(1)} %collective-permute-done.11), channel_id=1, source_target_pairs={{0,32},{32,0},{8,40},{40,8},{16,48},{48,16},{24,56},{56,24},{1,33}... | collective-permute-start | bytes 64520 | tf_op jit(solution)/shard_map/ppermute | solution.py:19
  305.6 1.5 copy-start.4
  307.1 8.6 %copy-start.28 = (f32[64,14,3]{2,0,1:T(8,128)S(1)}, f32[64,14,3]{2,0,1:T(8,128)}, u32[]{:S(2)}) copy-start(f32[64,14,3]{2,0,1:T(8,128)} %get-tuple-element.186) | copy-start | bytes 32260
  307.1 19.2 %collective-permute-start.13 = (f32[64,14,3]{2,0,1:T(8,128)}, f32[64,14,3]{2,0,1:T(8,128)}, u32[]{:S(2)}, u32[]{:S(2)}) collective-permute-start(f32[64,14,3]{2,0,1:T(8,128)} %get-tuple-element.187), channel_id=1, source_target_pairs={{0,1},{1,2},{2,3},{3,4},{4,5},{5,6},{6,7},{7,0},{8,9},{9,10},{10,1... | collective-permute-start | bytes 32264 | tf_op jit(solution)/shard_map/ppermute | solution.py:28
  315.6 15.8 %collective-permute-start.14 = (f32[64,14,3]{2,0,1:T(8,128)S(1)}, f32[64,14,3]{2,0,1:T(8,128)}, u32[]{:S(2)}, u32[]{:S(2)}) collective-permute-start(f32[64,14,3]{2,0,1:T(8,128)S(1)} %copy-done.28), channel_id=1, source_target_pairs={{1,0},{2,1},{3,2},{4,3},{5,4},{6,5},{7,6},{0,7},{9,8},{10,9},{11,1... | collective-permute-start | bytes 32264 | tf_op jit(solution)/shard_map/ppermute | solution.py:31
  338.9 2.5 copy-start.27
  339.7 2.4 copy-start.3
  339.7 2.4 copy-start.12
  339.7 2.4 copy-start.19
  341.4 373.6 %all-reduce.104.cloned.1.call-start = ((), (), s32[]{:S(2)}) async-start(), calls=%async_computation.5 | async-start | bytes 393216 | tf_op jit(solution)/shard_map/psum | solution.py:303
  345.1 1.7 copy-start.35
  345.1 1.7 copy-start.36
  345.1 1.7 copy-start.37
  345.1 1.7 copy-start.38
  345.1 1.7 copy-start.39
  345.2 1.7 copy-start.40
  345.2 1.7 copy-start.41
  345.2 1.7 copy-start.42
  345.2 1.8 copy-start.6
  345.2 1.8 copy-start.17
  345.2 1.8 copy-start.22
  345.2 102.2 %copy-start.8 = (f32[64,1024]{1,0:T(8,128)S(1)}, f32[64,1024]{1,0:T(8,128)}, u32[]{:S(2)}) copy-start(f32[64,1024]{1,0:T(8,128)} %copy-done.7) | copy-start | bytes 786436
  345.2 102.2 %copy-start.10 = (f32[64,1024]{1,0:T(8,128)S(1)}, f32[64,1024]{1,0:T(8,128)}, u32[]{:S(2)}) copy-start(f32[64,1024]{1,0:T(8,128)} %copy-done.9) | copy-start | bytes 786436
  346.8 102.6 %copy-start.14 = (bf16[256,1024]{0,1:T(8,128)(2,1)S(1)}, bf16[256,1024]{0,1:T(8,128)(2,1)}, u32[]{:S(2)}) copy-start(bf16[256,1024]{0,1:T(8,128)(2,1)} %copy-done.13) | copy-start | bytes 1572868
  346.8 102.6 %copy-start.20 = (bf16[128,1024]{1,0:T(8,128)(2,1)S(1)}, bf16[128,1024]{1,0:T(8,128)(2,1)}, u32[]{:S(2)}) copy-start(bf16[128,1024]{1,0:T(8,128)(2,1)} %copy-done.18) | copy-start | bytes 786436
  447.5 279.1 %copy-start.24 = (f32[8,8,8,128]{3,2,1,0:T(8,128)S(1)}, f32[8,8,8,128]{3,2,1,0:T(8,128)}, u32[]{:S(2)}) copy-start(f32[8,8,8,128]{3,2,1,0:T(8,128)} %get-tuple-element.192) | copy-start | bytes 786436
  453.0 263.4 %collective-permute-start.15 = (bf16[2,64,3,128]{3,1,2,0:T(8,128)(2,1)S(1)}, bf16[2,64,3,128]{3,1,2,0:T(8,128)(2,1)S(1)}, u32[]{:S(2)}, u32[]{:S(2)}) collective-permute-start(bf16[2,64,3,128]{3,1,2,0:T(8,128)(2,1)S(1)} %slice_bitcast_fusion.2), channel_id=1, source_target_pairs={{0,1},{1,0},{2,3},{3,2},{4,5},{5,4},{6,7},{7,6},{8,9},{9,8},{10,11... | collective-permute-start | bytes 294920 | tf_op jit(solution)/shard_map/ppermute | solution.py:19
  714.9 22.4 %copy-start.31 = (f32[128,128]{1,0:T(8,128)S(1)}, f32[128,128]{1,0:T(8,128)}, u32[]{:S(2)}) copy-start(f32[128,128]{1,0:T(8,128)} %get-tuple-element.179) | copy-start | bytes 196612
  716.4 8.2 %collective-permute-start.16 = (bf16[2,64,3,128]{3,1,2,0:T(8,128)(2,1)S(1)}, bf16[2,64,3,128]{3,1,2,0:T(8,128)(2,1)S(1)}, u32[]{:S(2)}, u32[]{:S(2)}) collective-permute-start(bf16[2,64,3,128]{3,1,2,0:T(8,128)(2,1)S(1)} %collective-permute-done.15), channel_id=1, source_target_pairs={{0,2},{2,0},{1,3},{3,1},{4,6},{6,4},{5,7},{7,5},{8,10},{10,8},{9,1... | collective-permute-start | bytes 294920 | tf_op jit(solution)/shard_map/ppermute | solution.py:19
  724.6 5.8 collective-permute-start.17
  731.5 6.5 collective-permute-start.18
  735.4 6.9 collective-permute-start.19
  (4 other events, 2.9 us)
Sparse Core Ops, SparseCore 0:
  43.2 44.4 all-gather.3
  186.4 91.3 reduce-scatter.2
  341.5 38.5 reduce-scatter.4
  452.2 262.6 all-reduce.103
where the time goes:
time: 751 us; the launch traced here: 750 us
  waiting for transfers between devices  427 us (57%)
  blocking collectives  118 us (16%)
  starting transfers between devices  87.2 us (12%)
  other arithmetic  46.3 us (6%)
  local copies, waits for them, and re-layouts  35.9 us (5%)
  between operations  20.2 us (3%)
  matrix products  14.7 us (2%)
    psum x1, waiting for transfers between devices, body(): lax.psum((kernel_grad, expand_grad, reduce_grad, gates_grad, candidate_gr...  258 us
    psum x1, blocking collectives, body(): lax.psum((kernel_grad, expand_grad, reduce_grad, gates_grad, candidate_gr...  99 us
    reduce_scatter x1, waiting for transfers between devices, seam_columns_backward(): lax.psum_scatter(terms.astype(jnp.bfloat16), 'face', scatter_dimension=0,...  91.5 us
    ppermute x12, starting transfers between devices, swapped(): return lax.ppermute(block, axis, route)  55.6 us
    all_gather x1, waiting for transfers between devices, seam_rows_forward(): lax.all_gather(stacked[None], 'face', axis=0, tiled=True)  36.8 us
    ppermute x12, waiting for transfers between devices, swapped(): return lax.ppermute(block, axis, route)  20.8 us
    ppermute x4, starting transfers between devices, padded_2(): lax.ppermute(lax.slice_in_dim(block, 0, width, axis=dim), axis, backward)  20.4 us
    all_gather x1, blocking collectives, seam_columns_forward(): lax.all_gather(stacked[None], 'face', axis=0, tiled=True)  19.1 us
  transfers between devices with their start and end apart: 24, of which 18 were waited for; matrix products, arithmetic and copies ran while one was open for 5% of the time, Pallas kernels for 0%

commit v1 on v0

v1 whole, which is shorter than its diff:
```python
import functools
import math

import jax
import jax.numpy as jnp
import numpy as np
from jax import lax
from jax.experimental import pallas as pl
from jax.experimental.pallas import tpu as pltpu
from jax.sharding import PartitionSpec as P

AXES = ("face", "row", "col")
CH = 64
HID = 256
KS = 7
RIM = 3
TR = 8
TC = 128
PR = TR + 2 * RIM
PACK_ROWS = 512
BF = jnp.bfloat16
F32 = jnp.float32
MESH = pl.DeviceIdType.MESH
VMEM = pl.BlockSpec(memory_space=pltpu.VMEM)
SMEM = pl.BlockSpec(memory_space=pltpu.SMEM)
LIMIT = 40 * 1024 * 1024


def spread_matrix():
    table = np.zeros((TC, PR * TC), np.float32)
    for row in range(PR):
        for i in range(6):
            table[row * 8 + i, row * TC + (i - RIM) % TC] = 1.0
    return table


def turn_matrices():
    table = np.zeros((4, TC, TC), np.float32)
    for code in range(4):
        for row in range(PR):
            for i in range(6):
                to_row = PR - 1 - row if code >= 2 else row
                to_i = 5 - i if code % 2 else i
                table[code, row * 8 + i, to_row * 8 + to_i] = 1.0
    return table


def dot(a, b):
    return jnp.dot(a, b, preferred_element_type=F32)


def dot_nt(a, b):
    return lax.dot_general(a, b, (((1,), (1,)), ((), ())), preferred_element_type=F32)


def send(src, dst, send_sem, recv_sem, device):
    return pltpu.make_async_remote_copy(
        src_ref=src,
        dst_ref=dst,
        send_sem=send_sem,
        recv_sem=recv_sem,
        device_id=device,
        device_id_type=MESH,
    )


def partner_of(seam_face, side, face, count):
    found = jnp.int32(0)
    for other in range(count):
        found = jnp.where(seam_face[other, side] == face, other, found)
    return found


def kind_of(side_bit, code):
    odd = lax.rem(code, 2)
    return jnp.where(side_bit == 0, 1 - odd, odd)


class Place:
    def __init__(self, dims):
        self.nf, self.nr, self.nc = dims
        self.f = lax.axis_index("face")
        self.r = lax.axis_index("row")
        self.c = lax.axis_index("col")
        self.top = self.r == 0
        self.bottom = self.r == self.nr - 1
        self.left = self.c == 0
        self.right = self.c == self.nc - 1
        self.row_edge = jnp.logical_or(self.top, self.bottom)
        self.col_edge = jnp.logical_or(self.left, self.right)
        self.row_kind = jnp.where(self.top, 0, 1)
        self.col_kind = jnp.where(self.left, 0, 1)

    def at(self, f=None, r=None, c=None):
        return (
            self.f if f is None else f,
            self.r if r is None else r,
            self.c if c is None else c,
        )

    def row_group(self):
        other_r = self.nr - 1 - self.r
        other_c = self.nc - 1 - self.c
        return [
            (self.at(c=other_c), self.row_kind * 2 + 1, self.row_kind * 2 + 1),
            (self.at(r=other_r), self.row_kind * 2, (1 - self.row_kind) * 2),
            (self.at(r=other_r, c=other_c), self.row_kind * 2 + 1, (1 - self.row_kind) * 2 + 1),
        ]

    def col_group(self):
        other_r = self.nr - 1 - self.r
        other_c = self.nc - 1 - self.c
        return [
            (self.at(r=other_r), self.col_kind * 2 + 1, self.col_kind * 2 + 1),
            (self.at(c=other_c), self.col_kind * 2, (1 - self.col_kind) * 2),
            (self.at(r=other_r, c=other_c), self.col_kind * 2 + 1, (1 - self.col_kind) * 2 + 1),
        ]

    def ring(self, axis):
        index, count = {"face": (self.f, self.nf), "row": (self.r, self.nr), "col": (self.c, self.nc)}[axis]
        out = []
        for step in range(1, count):
            other = lax.rem(index + step, count)
            out.append((other, self.at(**{axis[0]: other}), step))
        return out


def start_group(group, src, slots, sems, back):
    for i, (device, slot, unused) in enumerate(group):
        send(src, slots.at[slot], sems.at[back, i], sems.at[back + 1, slot], device).start()


def wait_group(group, src, slots, sems, back):
    for i, (device, unused, slot) in enumerate(group):
        send(src, slots.at[slot], sems.at[back, i], sems.at[back + 1, slot], device).wait_recv()


def done_group(group, src, slots, sems, back):
    for i, (device, unused, slot) in enumerate(group):
        send(src, slots.at[slot], sems.at[back, i], sems.at[back + 1, slot], device).wait_send()


def start_ring(ring, me, src_of, slots, sems):
    for other, device, step in ring:
        send(src_of(other), slots.at[me], sems.at[0, step], sems.at[1, me], device).start()


def wait_ring(ring, src_of, slots, sems):
    for other, device, step in ring:
        send(src_of(other), slots.at[other], sems.at[0, step], sems.at[1, other], device).wait_recv()


def done_ring(ring, src_of, slots, sems):
    for other, device, step in ring:
        send(src_of(other), slots.at[other], sems.at[0, step], sems.at[1, other], device).wait_send()


def greet(barrier, device):
    pl.semaphore_signal(barrier, inc=1, device_id=device, device_id_type=MESH)


def gather_kernel(
    dims,
    x_ref,
    spread_ref,
    turn_ref,
    flip_ref,
    sf,
    sc,
    xw_out,
    halo_out,
    xw,
    strips,
    chosen,
    faces,
    pack,
    sides,
    col_strips,
    col_chosen,
    col_faces,
    near,
    group_sem,
    row_face_sem,
    col_face_sem,
):
    at = Place(dims)
    nf, nr, nc = dims
    edge = jnp.logical_or(at.row_edge, at.col_edge)
    barrier = pltpu.get_barrier_semaphore()
    expected = (
        jnp.where(at.top, 0, 1)
        + jnp.where(at.bottom, 0, 1)
        + jnp.where(at.left, 0, 1)
        + jnp.where(at.right, 0, 1)
        + jnp.where(at.row_edge, 3, 0)
        + jnp.where(at.col_edge, 3, 0)
        + jnp.where(edge, nf - 1, 0)
    )
    above = at.at(r=jnp.maximum(at.r - 1, 0))
    below = at.at(r=jnp.minimum(at.r + 1, nr - 1))
    before = at.at(c=jnp.maximum(at.c - 1, 0))
    after = at.at(c=jnp.minimum(at.c + 1, nc - 1))
    has_above = jnp.logical_not(at.top)
    has_below = jnp.logical_not(at.bottom)
    has_before = jnp.logical_not(at.left)
    has_after = jnp.logical_not(at.right)
    for present, device in ((has_above, above), (has_below, below), (has_before, before), (has_after, after)):

        @pl.when(present)
        def _(device=device):
            greet(barrier, device)

    @pl.when(at.row_edge)
    def _():
        for device, unused, unused2 in at.row_group():
            greet(barrier, device)

    @pl.when(at.col_edge)
    def _():
        for device, unused, unused2 in at.col_group():
            greet(barrier, device)

    @pl.when(edge)
    def _():
        for unused, device, unused2 in at.ring("face"):
            greet(barrier, device)

    xw[RIM : RIM + TR] = x_ref[...]
    pl.semaphore_wait(barrier, expected)

    def to_above():
        return send(xw.at[pl.ds(RIM, RIM)], xw.at[pl.ds(RIM + TR, RIM)], near.at[0, 0], near.at[1, 0], above)

    def to_below():
        return send(xw.at[pl.ds(TR, RIM)], xw.at[pl.ds(0, RIM)], near.at[0, 1], near.at[1, 1], below)

    def own_edge():
        return xw.at[pl.ds(jnp.where(at.top, RIM, TR), RIM)]

    @pl.when(at.row_edge)
    def _():
        start_group(at.row_group(), own_edge(), strips, group_sem, 0)

    @pl.when(has_above)
    def _():
        to_above().start()

    @pl.when(has_below)
    def _():
        to_below().start()

    @pl.when(at.row_edge)
    def _():
        group = at.row_group()
        strips[at.row_kind * 2] = own_edge()[...]
        wait_group(group, own_edge(), strips, group_sem, 0)
        taker = partner_of(sf, at.row_kind, at.f, nf)
        code = sc[taker, at.row_kind]
        wanted = kind_of(at.row_kind, code) * 2 + code // 2
        picked = strips[wanted]
        chosen[...] = picked
        ring = at.ring("face")
        start_ring(ring, at.f, lambda other: chosen, faces, row_face_sem)
        faces[at.f] = picked
        wait_ring(ring, lambda other: chosen, faces, row_face_sem)
        code = sc[at.f, at.row_kind]
        strip = faces[sf[at.f, at.row_kind]].astype(F32)
        turned = jnp.concatenate([strip[2:3], strip[1:2], strip[0:1]], axis=0)
        strip = jnp.where(lax.rem(code, 2) == 1, turned, strip)
        mirrored = dot(strip.reshape(RIM * CH, TC).astype(BF), flip_ref[...]).reshape(RIM, CH, TC)
        strip = jnp.where(code >= 2, mirrored, strip)
        xw[pl.ds(jnp.where(at.top, 0, RIM + TR), RIM)] = strip.astype(BF)

    @pl.when(has_below)
    def _():
        to_above().wait_recv()

    @pl.when(has_above)
    def _():
        to_below().wait_recv()

    flat = jnp.concatenate([xw[row] for row in range(PR)], axis=1)
    pack[...] = dot_nt(flat, spread_ref[...]).astype(BF)

    def to_before():
        return send(pack, sides.at[1], near.at[0, 2], near.at[1, 2], before)

    def to_after():
        return send(pack, sides.at[0], near.at[0, 3], near.at[1, 3], after)

    @pl.when(at.col_edge)
    def _():
        start_group(at.col_group(), pack, col_strips, group_sem, 2)

    @pl.when(has_before)
    def _():
        to_before().start()

    @pl.when(has_after)
    def _():
        to_after().start()

    xw_out[...] = xw[...]

    @pl.when(at.col_edge)
    def _():
        group = at.col_group()
        col_strips[at.col_kind * 2] = pack[...]
        wait_group(group, pack, col_strips, group_sem, 2)
        taker = partner_of(sf, at.col_kind + 2, at.f, nf)
        code = sc[taker, at.col_kind + 2]
        wanted = kind_of(at.col_kind, code) * 2 + code // 2
        picked = col_strips[wanted]
        col_chosen[...] = picked
        ring = at.ring("face")
        start_ring(ring, at.f, lambda other: col_chosen, col_faces, col_face_sem)
        col_faces[at.f] = picked
        wait_ring(ring, lambda other: col_chosen, col_faces, col_face_sem)
        code = sc[at.f, at.col_kind + 2]
        strip = col_faces[sf[at.f, at.col_kind + 2]]
        sides[at.col_kind] = dot(strip, turn_ref[code]).astype(BF)

    @pl.when(has_after)
    def _():
        to_before().wait_recv()

    @pl.when(has_before)
    def _():
        to_after().wait_recv()

    place = lax.rem(lax.broadcasted_iota(jnp.int32, (CH, TC), 1), 8)
    halo_out[...] = jnp.where(place < RIM, sides[0].astype(F32), sides[1].astype(F32)).astype(BF)

    @pl.when(has_above)
    def _():
        to_above().wait_send()

    @pl.when(has_below)
    def _():
        to_below().wait_send()

    @pl.when(has_before)
    def _():
        to_before().wait_send()

    @pl.when(has_after)
    def _():
        to_after().wait_send()

    @pl.when(at.row_edge)
    def _():
        done_group(at.row_group(), own_edge(), strips, group_sem, 0)
        done_ring(at.ring("face"), lambda other: chosen, faces, row_face_sem)

    @pl.when(at.col_edge)
    def _():
        done_group(at.col_group(), pack, col_strips, group_sem, 2)
        done_ring(at.ring("face"), lambda other: col_chosen, col_faces, col_face_sem)


def tile_kernel(
    xw_ref,
    halo_ref,
    prior_ref,
    cot_ref,
    kernel_ref,
    we_ref,
    wr_ref,
    wg_ref,
    wc_ref,
    spread_ref,
    next_ref,
    prior_grad_ref,
    main_ref,
    rim_ref,
    grads_ref,
    xf,
    ef,
    shifted,
    taps,
    summed,
    back,
    prior,
    cot,
    after,
    prior_grad,
    edge_grad,
    ge,
    gr,
    gg,
    gc,
):
    xf[...] = xw_ref[...].astype(F32)
    ends = dot(halo_ref[...], spread_ref[...])
    for row in range(PR):
        ef[row] = ends[:, row * TC : (row + 1) * TC]
    prior[...] = prior_ref[...].astype(F32).reshape(CH * TR, TC)
    cot[...] = cot_ref[...].astype(F32).reshape(CH * TR, TC)
    lane = lax.broadcasted_iota(jnp.int32, (8, TC), 1)

    def forward(g, carry):
        part = pl.ds(pl.multiple_of(g * 8, 8), 8)
        values = kernel_ref[part, :]
        total = [jnp.zeros((8, TC), F32)] * TR
        for b in range(KS):
            d = b - RIM
            rows = []
            for row in range(PR):
                value = xf[row, part, :]
                if d > 0:
                    value = jnp.where(lane < d, ef[row, part, :], value)
                elif d < 0:
                    value = jnp.where(lane >= TC + d, ef[row, part, :], value)
                if d:
                    value = pltpu.roll(value, (-d) % TC, 1)
                shifted[b, row, part, :] = value
                rows.append(value)
            for a in range(KS):
                tap = a * KS + b
                weight = jnp.broadcast_to(values[:, tap : tap + 1], (8, TC))
                taps[tap, part, :] = weight
                for y in range(TR):
                    total[y] = total[y] + weight * rows[y + a]
        for y in range(TR):
            summed[y, part, :] = total[y]
        return carry

    lax.fori_loop(0, CH // 8, forward, 0)

    we = we_ref[...]
    wr = wr_ref[...]
    wg = wg_ref[...]
    wc = wc_ref[...]
    we_t = we.T
    wr_t = wr.T
    wg_t = wg.T
    wc_t = wc.T
    for ref in (ge, gr, gg, gc):
        ref[...] = jnp.zeros_like(ref)

    def chunk(i, carry):
        r0 = i * 2

        def pair(load):
            return jnp.concatenate([load(r0), load(r0 + 1)], axis=1)

        s = pair(lambda y: summed[y])
        center = s - jnp.mean(s, axis=0, keepdims=True)
        scale = lax.rsqrt(jnp.mean(center * center, axis=0, keepdims=True) + 1e-06)
        unit = center * scale
        normed = unit.astype(BF)
        hidden = dot(we_t, normed)
        acts = []
        slopes = []
        for start in range(0, HID, 32):
            h = hidden[start : start + 32]
            cdf = 0.5 + 0.5 * lax.erf(h * math.sqrt(0.5))
            acts.append((h * cdf).astype(BF))
            slopes.append(cdf + h * (jnp.exp(-0.5 * h * h) * (1.0 / math.sqrt(2.0 * math.pi))))
        act = jnp.concatenate(acts, axis=0)
        slope = jnp.concatenate(slopes, axis=0)
        out = (pair(lambda y: xf[RIM + y]) + dot(wr_t, act)).astype(BF)
        before = pair(lambda y: prior[pl.ds(y, CH, stride=TR), :])
        joined = jnp.concatenate([out, before.astype(BF)], axis=0)
        gates = jax.nn.sigmoid(dot(wg_t, joined))
        update = gates[:CH]
        reset = gates[CH:]
        joined_reset = jnp.concatenate([out, (reset * before).astype(BF)], axis=0)
        proposal = jnp.tanh(dot(wc_t, joined_reset))
        result = (1.0 - update) * before + update * proposal
        g = pair(lambda y: cot[pl.ds(y, CH, stride=TR), :])
        d_cand = (g * update * (1.0 - proposal * proposal)).astype(BF)
        d_joined_reset = dot(wc, d_cand)
        d_reset = d_joined_reset[CH:]
        d_gates = jnp.concatenate(
            [
                g * (proposal - before) * (update * (1.0 - update)),
                d_reset * before * (reset * (1.0 - reset)),
            ],
            axis=0,
        ).astype(BF)
        d_joined = dot(wg, d_gates)
        d_out = (d_joined_reset[:CH] + d_joined[:CH]).astype(BF)
        d_prior = g * (1.0 - update) + d_reset * reset + d_joined[CH:]
        d_hidden = (dot(wr, d_out) * slope).astype(BF)
        d_normed = dot(we, d_hidden)
        ge[...] += dot_nt(normed, d_hidden)
        gr[...] += dot_nt(d_out, act)
        gg[...] += dot_nt(joined, d_gates)
        gc[...] += dot_nt(d_cand, joined_reset)
        d_summed = scale * (
            d_normed
            - jnp.mean(d_normed, axis=0, keepdims=True)
            - unit * jnp.mean(d_normed * unit, axis=0, keepdims=True)
        )
        d_center = d_out.astype(F32)
        for j in range(2):
            y = r0 + j
            cut = slice(j * TC, (j + 1) * TC)
            back[y] = d_summed[:, cut]
            main_ref[RIM + y] = d_center[:, cut]
            after[pl.ds(y, CH, stride=TR), :] = result[:, cut]
            prior_grad[pl.ds(y, CH, stride=TR), :] = d_prior[:, cut]
        return carry

    lax.fori_loop(0, TR // 2, chunk, 0)
    next_ref[...] = after[...].reshape(CH, TR, TC).astype(BF)
    prior_grad_ref[...] = prior_grad[...].reshape(CH, TR, TC).astype(BF)
    grads_ref[0:64] = ge[:, :TC].astype(BF)
    grads_ref[64:128] = ge[:, TC:].astype(BF)
    grads_ref[128:192] = gr[:, :TC].astype(BF)
    grads_ref[192:256] = gr[:, TC:].astype(BF)
    grads_ref[256:384] = gg[...].astype(BF)
    grads_ref[384:448] = gc[...].astype(BF)

    def backward(g, carry):
        part = pl.ds(pl.multiple_of(g * 8, 8), 8)
        rows = [back[y, part, :] for y in range(TR)]
        inner = [jnp.zeros((8, TC), F32)] * PR
        outer = [jnp.zeros((8, TC), F32)] * PR
        kernel_grad = jnp.zeros((8, TC), F32)
        for b in range(KS):
            d = b - RIM
            columns = [None] * PR
            for a in range(KS):
                tap = a * KS + b
                weight = taps[tap, part, :]
                terms = None
                for y in range(TR):
                    product = weight * rows[y]
                    columns[y + a] = product if columns[y + a] is None else columns[y + a] + product
                    term = rows[y] * shifted[b, y + a, part, :]
                    terms = term if terms is None else terms + term
                kernel_grad = jnp.where(lane == tap, jnp.sum(terms, axis=1, keepdims=True), kernel_grad)
            for row in range(PR):
                if d == 0:
                    inner[row] = inner[row] + columns[row]
                    continue
                moved = pltpu.roll(columns[row], d % TC, 1)
                wrapped = lane < d if d > 0 else lane >= TC + d
                inner[row] = inner[row] + jnp.where(wrapped, 0.0, moved)
                outer[row] = outer[row] + jnp.where(wrapped, moved, 0.0)
        for row in range(PR):
            if RIM <= row < RIM + TR:
                main_ref[row, part, :] = main_ref[row, part, :] + inner[row]
            else:
                main_ref[row, part, :] = inner[row]
            edge_grad[row, part, :] = outer[row]
        gc[part, :] = kernel_grad
        return carry

    lax.fori_loop(0, CH // 8, backward, 0)
    grads_ref[448:512] = gc[...].astype(BF)
    flat = jnp.concatenate([edge_grad[row] for row in range(PR)], axis=1).astype(BF)
    rim_ref[...] = dot_nt(flat, spread_ref[...]).astype(BF)


def return_kernel(
    dims,
    main_ref,
    rim_ref,
    grads_ref,
    spread_ref,
    turn_ref,
    flip_ref,
    sf,
    sc,
    input_out,
    grads_out,
    total,
    edges,
    sides,
    col_faces,
    col_chosen,
    col_strips,
    row_sides,
    row_faces,
    row_chosen,
    row_strips,
    a1,
    a2_src,
    a2,
    a3_src,
    a3,
    a4_src,
    a4,
    a5_src,
    a5,
    near,
    group_sem,
    col_face_sem,
    row_face_sem,
    s1,
    s2,
    s3,
    s4,
    s5,
):
    at = Place(dims)
    nf, nr, nc = dims
    part1 = PACK_ROWS // nf
    part2 = part1 // nc
    barrier = pltpu.get_barrier_semaphore()
    face_ring = at.ring("face")
    row_ring = at.ring("row")
    col_ring = at.ring("col")
    for ring in (face_ring, row_ring, col_ring):
        for unused, device, unused2 in ring:
            greet(barrier, device)
    corner = at.at(r=nr - 1 - at.r, c=nc - 1 - at.c)
    any_edge = jnp.logical_or(at.row_edge, at.col_edge)

    @pl.when(any_edge)
    def _():
        greet(barrier, corner)

    pl.semaphore_wait(barrier, nf + nr + nc - 3 + jnp.where(any_edge, 1, 0))

    above = at.at(r=jnp.maximum(at.r - 1, 0))
    below = at.at(r=jnp.minimum(at.r + 1, nr - 1))
    before = at.at(c=jnp.maximum(at.c - 1, 0))
    after = at.at(c=jnp.minimum(at.c + 1, nc - 1))
    has_above = jnp.logical_not(at.top)
    has_below = jnp.logical_not(at.bottom)
    has_before = jnp.logical_not(at.left)
    has_after = jnp.logical_not(at.right)

    def to_before():
        return send(rim_ref, sides.at[1], near.at[0, 2], near.at[1, 2], before)

    def to_after():
        return send(rim_ref, sides.at[0], near.at[0, 3], near.at[1, 3], after)

    @pl.when(at.col_edge)
    def _():
        start_ring(face_ring, at.f, lambda other: rim_ref, col_faces, col_face_sem)

    @pl.when(has_before)
    def _():
        to_before().start()

    @pl.when(has_after)
    def _():
        to_after().start()

    def piece1(other):
        return grads_ref.at[pl.ds(pl.multiple_of(other * part1, part1), part1)]

    start_ring(face_ring, at.f, piece1, a1, s1)
    a1[at.f] = piece1(at.f)[...]

    place = lax.rem(lax.broadcasted_iota(jnp.int32, (CH, TC), 1), 8)
    low = place < RIM

    @pl.when(at.col_edge)
    def _():
        side = at.col_kind + 2
        col_faces[at.f] = rim_ref[...]
        wait_ring(face_ring, lambda other: rim_ref, col_faces, col_face_sem)
        taker = partner_of(sf, side, at.f, nf)
        strip = col_faces[taker].astype(F32)
        strip = jnp.where(low == at.left, strip, 0.0).astype(BF)
        turned = dot(strip, turn_ref[sc[taker, side]]).astype(BF)
        col_chosen[...] = turned
        start_group(at.col_group(), col_chosen, col_strips, group_sem, 0)
        col_strips[at.col_kind * 2] = turned

    wait_ring(face_ring, piece1, a1, s1)
    partial = a1[0].astype(F32)
    for other in range(1, nf):
        partial = partial + a1[other].astype(F32)
    a2_src[...] = partial

    def piece2(other):
        return a2_src.at[pl.ds(pl.multiple_of(other * part2, part2), part2)]

    start_ring(col_ring, at.c, piece2, a2, s2)
    a2[at.c] = piece2(at.c)[...]

    def seam_total(strips, kind, first_side):
        gathered = None
        for side_bit in range(2):
            taker = partner_of(sf, first_side + side_bit, at.f, nf)
            code = sc[taker, first_side + side_bit]
            mine = kind_of(side_bit, code) == kind
            for mirror in range(2):
                use = jnp.logical_and(mine, code // 2 == mirror)
                term = jnp.where(use, strips[side_bit * 2 + mirror].astype(F32), 0.0)
                gathered = term if gathered is None else gathered + term
        return gathered

    @pl.when(at.col_edge)
    def _():
        wait_group(at.col_group(), col_chosen, col_strips, group_sem, 0)
        sides[at.col_kind] = seam_total(col_strips, at.col_kind, 2).astype(BF)

    @pl.when(has_after)
    def _():
        to_before().wait_recv()

    @pl.when(has_before)
    def _():
        to_after().wait_recv()

    rim = jnp.where(low, sides[1].astype(F32), sides[0].astype(F32)).astype(BF)
    spread = dot(rim, spread_ref[...])
    for row in range(PR):
        total[row] = main_ref[row] + spread[:, row * TC : (row + 1) * TC]
    edges[0] = total[0:RIM].astype(BF)
    edges[1] = total[RIM + TR : PR].astype(BF)

    def to_above():
        return send(edges.at[0], row_sides.at[1], near.at[0, 0], near.at[1, 0], above)

    def to_below():
        return send(edges.at[1], row_sides.at[0], near.at[0, 1], near.at[1, 1], below)

    def own_edge():
        return edges.at[at.row_kind]

    @pl.when(at.row_edge)
    def _():
        start_ring(face_ring, at.f, lambda other: own_edge(), row_faces, row_face_sem)

    @pl.when(has_above)
    def _():
        to_above().start()

    @pl.when(has_below)
    def _():
        to_below().start()

    wait_ring(col_ring, piece2, a2, s2)
    partial = a2[0]
    for other in range(1, nc):
        partial = partial + a2[other]
    a3_src[...] = partial
    start_ring(row_ring, at.r, lambda other: a3_src, a3, s3)
    a3[at.r] = partial

    @pl.when(at.row_edge)
    def _():
        row_faces[at.f] = own_edge()[...]
        wait_ring(face_ring, lambda other: own_edge(), row_faces, row_face_sem)
        taker = partner_of(sf, at.row_kind, at.f, nf)
        code = sc[taker, at.row_kind]
        strip = row_faces[taker].astype(F32)
        turned = jnp.concatenate([strip[2:3], strip[1:2], strip[0:1]], axis=0)
        strip = jnp.where(lax.rem(code, 2) == 1, turned, strip)
        mirrored = dot(strip.reshape(RIM * CH, TC).astype(BF), flip_ref[...]).reshape(RIM, CH, TC)
        strip = jnp.where(code >= 2, mirrored, strip).astype(BF)
        row_chosen[...] = strip
        start_group(at.row_group(), row_chosen, row_strips, group_sem, 2)
        row_strips[at.row_kind * 2] = strip

    wait_ring(row_ring, lambda other: a3_src, a3, s3)
    partial = a3[0]
    for other in range(1, nr):
        partial = partial + a3[other]
    a4_src[...] = partial
    start_ring(col_ring, at.c, lambda other: a4_src, a4, s4)
    a4[at.c] = partial

    @pl.when(at.row_edge)
    def _():
        wait_group(at.row_group(), row_chosen, row_strips, group_sem, 2)
        gathered = seam_total(row_strips, at.row_kind, 0)
        spot = pl.ds(jnp.where(at.top, RIM, TR), RIM)
        total[spot] = total[spot] + gathered

    @pl.when(has_below)
    def _():
        to_above().wait_recv()
        total[TR : TR + RIM] = total[TR : TR + RIM] + row_sides[1].astype(F32)

    @pl.when(has_above)
    def _():
        to_below().wait_recv()
        total[RIM : 2 * RIM] = total[RIM : 2 * RIM] + row_sides[0].astype(F32)

    wait_ring(col_ring, lambda other: a4_src, a4, s4)
    full = jnp.concatenate([a4[other] for other in range(nc)], axis=0).astype(BF)
    a5_src[...] = full
    start_ring(face_ring, at.f, lambda other: a5_src, a5, s5)
    a5[at.f] = full
    input_out[...] = total[RIM : RIM + TR].astype(BF)
    wait_ring(face_ring, lambda other: a5_src, a5, s5)
    for other in range(nf):
        grads_out[other * part1 : (other + 1) * part1] = a5[other]

    @pl.when(has_above)
    def _():
        to_above().wait_send()

    @pl.when(has_below)
    def _():
        to_below().wait_send()

    @pl.when(has_before)
    def _():
        to_before().wait_send()

    @pl.when(has_after)
    def _():
        to_after().wait_send()

    @pl.when(at.col_edge)
    def _():
        done_ring(face_ring, lambda other: rim_ref, col_faces, col_face_sem)
        done_group(at.col_group(), col_chosen, col_strips, group_sem, 0)

    @pl.when(at.row_edge)
    def _():
        done_ring(face_ring, lambda other: own_edge(), row_faces, row_face_sem)
        done_group(at.row_group(), row_chosen, row_strips, group_sem, 2)

    done_ring(face_ring, piece1, a1, s1)
    done_ring(col_ring, piece2, a2, s2)
    done_ring(row_ring, lambda other: a3_src, a3, s3)
    done_ring(col_ring, lambda other: a4_src, a4, s4)
    done_ring(face_ring, lambda other: a5_src, a5, s5)


def tile_step(xw, halo, prior, cot, kernel, we, wr, wg, wc, spread):
    tile = jax.ShapeDtypeStruct((CH, TR, TC), BF)
    wide = (PR, CH, TC)
    return pl.pallas_call(
        tile_kernel,
        out_shape=(
            tile,
            tile,
            jax.ShapeDtypeStruct(wide, F32),
            jax.ShapeDtypeStruct((CH, TC), BF),
            jax.ShapeDtypeStruct((PACK_ROWS, TC), BF),
        ),
        in_specs=[VMEM] * 10,
        out_specs=(VMEM,) * 5,
        scratch_shapes=[
            pltpu.VMEM(wide, F32),
            pltpu.VMEM(wide, F32),
            pltpu.VMEM((KS,) + wide, F32),
            pltpu.VMEM((KS * KS, CH, TC), F32),
            pltpu.VMEM((TR, CH, TC), F32),
            pltpu.VMEM((TR, CH, TC), F32),
            pltpu.VMEM((CH * TR, TC), F32),
            pltpu.VMEM((CH * TR, TC), F32),
            pltpu.VMEM((CH * TR, TC), F32),
            pltpu.VMEM((CH * TR, TC), F32),
            pltpu.VMEM(wide, F32),
            pltpu.VMEM((CH, HID), F32),
            pltpu.VMEM((CH, HID), F32),
            pltpu.VMEM((2 * CH, 2 * CH), F32),
            pltpu.VMEM((CH, 2 * CH), F32),
        ],
        compiler_params=pltpu.CompilerParams(vmem_limit_bytes=LIMIT),
        name="tile_step",
    )(xw, halo, prior, cot, kernel, we, wr, wg, wc, spread)


def dma(*shape):
    return pltpu.SemaphoreType.DMA(shape)


def gather_halos(dims, rows, spread, turn, flip, sf, sc):
    nf = dims[0]
    strip = (RIM, CH, TC)
    return pl.pallas_call(
        functools.partial(gather_kernel, dims),
        out_shape=(
            jax.ShapeDtypeStruct((PR, CH, TC), BF),
            jax.ShapeDtypeStruct((CH, TC), BF),
        ),
        in_specs=[VMEM] * 4 + [SMEM] * 2,
        out_specs=(VMEM, VMEM),
        scratch_shapes=[
            pltpu.VMEM((PR, CH, TC), BF),
            pltpu.VMEM((4,) + strip, BF),
            pltpu.VMEM(strip, BF),
            pltpu.VMEM((nf,) + strip, BF),
            pltpu.VMEM((CH, TC), BF),
            pltpu.VMEM((2, CH, TC), BF),
            pltpu.VMEM((4, CH, TC), BF),
            pltpu.VMEM((CH, TC), BF),
            pltpu.VMEM((nf, CH, TC), BF),
            dma(2, 4),
            dma(4, 4),
            dma(2, nf),
            dma(2, nf),
        ],
        compiler_params=pltpu.CompilerParams(
            collective_id=0, has_side_effects=True, vmem_limit_bytes=LIMIT
        ),
        name="gather_halos",
    )(rows, spread, turn, flip, sf, sc)


def return_grads(dims, main, rim, grads, spread, turn, flip, sf, sc):
    nf, nr, nc = dims
    strip = (RIM, CH, TC)
    part1 = PACK_ROWS // nf
    part2 = part1 // nc
    return pl.pallas_call(
        functools.partial(return_kernel, dims),
        out_shape=(
            jax.ShapeDtypeStruct((TR, CH, TC), BF),
            jax.ShapeDtypeStruct((PACK_ROWS, TC), BF),
        ),
        in_specs=[VMEM] * 6 + [SMEM] * 2,
        out_specs=(VMEM, VMEM),
        scratch_shapes=[
            pltpu.VMEM((PR, CH, TC), F32),
            pltpu.VMEM((2,) + strip, BF),
            pltpu.VMEM((2, CH, TC), BF),
            pltpu.VMEM((nf, CH, TC), BF),
            pltpu.VMEM((CH, TC), BF),
            pltpu.VMEM((4, CH, TC), BF),
            pltpu.VMEM((2,) + strip, BF),
            pltpu.VMEM((nf,) + strip, BF),
            pltpu.VMEM(strip, BF),
            pltpu.VMEM((4,) + strip, BF),
            pltpu.VMEM((nf, part1, TC), BF),
            pltpu.VMEM((part1, TC), F32),
            pltpu.VMEM((nc, part2, TC), F32),
            pltpu.VMEM((part2, TC), F32),
            pltpu.VMEM((nr, part2, TC), F32),
            pltpu.VMEM((part2, TC), F32),
            pltpu.VMEM((nc, part2, TC), F32),
            pltpu.VMEM((part1, TC), BF),
            pltpu.VMEM((nf, part1, TC), BF),
            dma(2, 4),
            dma(4, 4),
            dma(2, nf),
            dma(2, nf),
            dma(2, nf),
            dma(2, nc),
            dma(2, nr),
            dma(2, nc),
            dma(2, nf),
        ],
        compiler_params=pltpu.CompilerParams(
            collective_id=1, has_side_effects=True, vmem_limit_bytes=LIMIT
        ),
        name="return_grads",
    )(main, rim, grads, spread, turn, flip, sf, sc)


def body(dims, cell_total, block_in, hidden_state, state_cotangent, kernel, we, wr, wg, wc, sf, sc):
    spread = jnp.asarray(spread_matrix(), BF)
    turn = jnp.asarray(turn_matrices(), BF)
    flip = jnp.asarray(np.eye(TC, dtype=np.float32)[::-1].copy(), BF)
    rows = jnp.transpose(block_in[0], (1, 0, 2))
    xw, halo = gather_halos(dims, rows, spread, turn, flip, sf, sc)
    next_state, prior_grad, main, rim, grads = tile_step(
        xw, halo, hidden_state[0], state_cotangent[0], kernel, we, wr, wg, wc, spread
    )
    input_grad, summed = return_grads(dims, main, rim, grads, spread, turn, flip, sf, sc)
    summed = summed.astype(F32) * (1.0 / math.sqrt(cell_total))
    halves = summed.reshape(8, CH, TC)
    return (
        next_state[None],
        jnp.transpose(input_grad, (1, 0, 2))[None],
        prior_grad[None],
        halves[7][:, : KS * KS],
        jnp.concatenate([halves[0], halves[1]], axis=1),
        jnp.concatenate([halves[2], halves[3]], axis=1).T,
        summed[256:384],
        halves[6].T,
    )


def solution(mesh):
    dims = tuple(mesh.shape[name] for name in AXES)
    cell_total = dims[0] * dims[1] * dims[2] * TR * TC
    tiles = P("face", None, "row", "col")
    return jax.shard_map(
        functools.partial(body, dims, cell_total),
        mesh=mesh,
        in_specs=(tiles,) * 3 + (P(),) * 7,
        out_specs=(tiles,) * 3 + (P(),) * 5,
        check_vma=False,
    )
```

time: 751 us -> 102 us (0.14)
  the two profiles are of different devices: /device:TPU:1 before, /device:TPU:2 now
where the time goes in v1:
time: 102 us; the launch traced here: 101 us
  Pallas kernels  91.2 us (89%)
  local copies, waits for them, and re-layouts  8.67 us (8%)
    pallas_call x1, Pallas kernels, return_grads(): pl.pallas_call(functools.partial(return_kernel, dims), out_shape=(jax.Sha...  48.4 us
    pallas_call x1, Pallas kernels, gather_halos(): pl.pallas_call(functools.partial(gather_kernel, dims), out_shape=(jax.Sha...  31.2 us
    pallas_call x1, Pallas kernels, tile_step(): pl.pallas_call(tile_kernel, out_shape=(tile, tile, jax.ShapeDtypeStruct(w...  11.5 us
    unnamed x22, local copies, waits for them, and re-layouts  7.4 us

profile of v1, /device:TPU:2, one launch (start us, length us, event | category | flops | bytes accessed | tf_op | source)
XLA Modules:
  0.0 101.3 jit_solution(360577731541619474)
XLA Ops:
  0.6 0.0 copy-start
  0.6 0.8 copy.22.sf
  1.5 0.8 copy.23.sc
  2.2 0.8 copy.24.kernel_ref
  3.0 0.8 copy.26.wc_ref
  3.9 0.9 copy.25.wr_ref
  4.8 0.0 copy-start.4
  4.8 0.9 copy.32
  5.7 0.0 copy-done
  5.7 0.0 copy-done.4
  5.7 0.0 copy-start.1
  5.7 0.9 copy-done.1
  6.6 0.0 copy-start.2
  6.6 0.0 copy-start.3
  6.6 0.0 copy-start.5
  6.6 0.0 copy-start.6
  6.6 31.2 %gather_halos.1 = (bf16[14,64,128]{2,1,0:T(8,128)(2,1)S(1)}, bf16[64,128]{1,0:T(8,128)(2,1)S(1)}) custom-call(bf16[8,64,128]{2,1,0:T(8,128)(2,1)S(1)} %bitcast.16, bf16[128,1792]{1,0:T(8,128)(2,1)S(1)} %copy-done, bf16[4,128,128]{2,1,0:T(8,128)(2,1)S(1)} %copy-done.1, bf16[128,128]{1,0:T(8,128)(2,1)S(1)} %copy-done.4, s32[8,4]{1,0:T(8,128)S(1)} %copy.22.sf, ...), custom_call_target="tpu_custom_call" | custom-call | tf_op jit(solution)/shard_map/gather_halos/pallas_call | solution.py:867
  37.9 0.0 copy-done.2
  37.9 0.0 copy-done.3
  37.9 0.0 copy-done.5
  37.9 0.0 copy-done.6
  37.9 11.5 %tile_step.1 = (bf16[64,8,128]{2,1,0:T(8,128)(2,1)}, bf16[64,8,128]{2,1,0:T(8,128)(2,1)}, f32[14,64,128]{2,1,0:T(8,128)S(1)}, bf16[64,128]{1,0:T(8,128)(2,1)S(1)}, bf16[512,128]{1,0:T(8,128)(2,1)S(1)}) custom-call(bf16[14,64,128]{2,1,0:T(8,128)(2,1)S(1)} %get-tuple-element.17.xw_ref, bf16[64,128]{1,0:T(8,128)(2,1)S(1)} %get-tuple-element.18.halo_ref, ...), custom_call_target="tpu_custom_call" | custom-call | tf_op jit(solution)/shard_map/tile_step/pallas_call | solution.py:827
  49.5 48.4 %return_grads.1 = (bf16[8,64,128]{2,1,0:T(8,128)(2,1)S(1)}, bf16[512,128]{1,0:T(8,128)(2,1)S(1)}) custom-call(f32[14,64,128]{2,1,0:T(8,128)S(1)} %get-tuple-element.20.main_ref, bf16[64,128]{1,0:T(8,128)(2,1)S(1)} %get-tuple-element.21.rim_ref, bf16[512,128]{1,0:T(8,128)(2,1)S(1)} %get-tuple-element.22.grads_ref, bf16[128,1792]{1,0:T(8,128)(2,1)S(1)} %copy-done, ...), custom_call_target="tpu_custom_call" | custom-call | tf_op jit(solution)/shard_map/return_grads/pallas_call | solution.py:902
  97.9 0.7 copy.29
  98.7 0.7 copy.30
  99.4 0.6 slice.41
  100.0 0.6 slice_bitcast_fusion
  100.6 0.7 pad_maximum_fusion
  (2 shorter events, 0.0 us)
Async XLA Ops:
  0.6 5.1 %copy-start = (bf16[128,1792]{1,0:T(8,128)(2,1)S(1)}, bf16[128,1792]{1,0:T(8,128)(2,1)}, u32[]{:S(2)}) copy-start(bf16[128,1792]{1,0:T(8,128)(2,1)} %constant.8.clone.spread_ref) | copy-start | bytes 1376260
  4.8 1.0 copy-start.4
  5.7 0.9 copy-start.1
  6.6 31.3 %copy-start.2 = (bf16[1,64,8,128]{3,2,1,0:T(8,128)(2,1)S(1)}, bf16[1,64,8,128]{3,2,1,0:T(8,128)(2,1)}, u32[]{:S(2)}) copy-start(bf16[1,64,8,128]{3,2,1,0:T(8,128)(2,1)} %param.14) | copy-start | bytes 393220
  6.6 31.3 %copy-start.3 = (bf16[1,64,8,128]{3,2,1,0:T(8,128)(2,1)S(1)}, bf16[1,64,8,128]{3,2,1,0:T(8,128)(2,1)}, u32[]{:S(2)}) copy-start(bf16[1,64,8,128]{3,2,1,0:T(8,128)(2,1)} %param.15) | copy-start | bytes 393220
  6.6 31.3 %copy-start.5 = (bf16[64,256]{1,0:T(8,128)(2,1)S(1)}, bf16[64,256]{1,0:T(8,128)(2,1)}, u32[]{:S(2)}) copy-start(bf16[64,256]{1,0:T(8,128)(2,1)} %we_ref.1) | copy-start | bytes 98308
  6.6 31.3 %copy-start.6 = (bf16[128,128]{1,0:T(8,128)(2,1)S(1)}, bf16[128,128]{1,0:T(8,128)(2,1)}, u32[]{:S(2)}) copy-start(bf16[128,128]{1,0:T(8,128)(2,1)} %wg_ref.1) | copy-start | bytes 98308

commit v2 on v1

v2 whole, which is shorter than its diff:
```python
import functools
import math

import jax
import jax.numpy as jnp
from jax import lax
from jax.experimental import pallas as pl
from jax.experimental.pallas import tpu as pltpu
from jax.sharding import PartitionSpec as P

AXES = ("face", "row", "col")
CH = 64
HID = 256
KS = 7
RIM = 3
TR = 8
TC = 128
PR = TR + 2 * RIM
PACK_ROWS = 512
BF = jnp.bfloat16
F32 = jnp.float32
MESH = pl.DeviceIdType.MESH
VMEM = pl.BlockSpec(memory_space=pltpu.VMEM)
SMEM = pl.BlockSpec(memory_space=pltpu.SMEM)
LIMIT = 40 * 1024 * 1024


def spread_block(row):
    source = lax.broadcasted_iota(jnp.int32, (TC, TC), 0)
    lane = lax.broadcasted_iota(jnp.int32, (TC, TC), 1)
    place = jnp.where(lane >= TC - RIM, lane - (TC - RIM), jnp.where(lane < RIM, lane + RIM, -TC * 8))
    return jnp.where(source == row * 8 + place, 1.0, 0.0).astype(BF)


def turn_matrix(code):
    source = lax.broadcasted_iota(jnp.int32, (TC, TC), 0)
    lane = lax.broadcasted_iota(jnp.int32, (TC, TC), 1)
    row = lane // 8
    place = lane % 8
    from_row = jnp.where(code >= 2, PR - 1 - row, row)
    from_place = jnp.where(code % 2 == 1, 5 - place, place)
    used = jnp.logical_and(place < 2 * RIM, row < PR)
    return jnp.where(jnp.where(used, from_row * 8 + from_place, -1) == source, 1.0, 0.0).astype(BF)


def flip_matrix():
    source = lax.broadcasted_iota(jnp.int32, (TC, TC), 0)
    lane = lax.broadcasted_iota(jnp.int32, (TC, TC), 1)
    return jnp.where(source == TC - 1 - lane, 1.0, 0.0).astype(BF)


def dot(a, b):
    return jnp.dot(a, b, preferred_element_type=F32)


def dot_nt(a, b):
    return lax.dot_general(a, b, (((1,), (1,)), ((), ())), preferred_element_type=F32)


def send(src, dst, send_sem, recv_sem, device):
    return pltpu.make_async_remote_copy(
        src_ref=src,
        dst_ref=dst,
        send_sem=send_sem,
        recv_sem=recv_sem,
        device_id=device,
        device_id_type=MESH,
    )


def partner_of(seam_face, side, face, count):
    found = jnp.int32(0)
    for other in range(count):
        found = jnp.where(seam_face[side, other] == face, other, found)
    return found


def kind_of(side_bit, code):
    odd = lax.rem(code, 2)
    return jnp.where(side_bit == 0, 1 - odd, odd)


class Place:
    def __init__(self, dims):
        self.nf, self.nr, self.nc = dims
        self.f = lax.axis_index("face")
        self.r = lax.axis_index("row")
        self.c = lax.axis_index("col")
        self.top = self.r == 0
        self.bottom = self.r == self.nr - 1
        self.left = self.c == 0
        self.right = self.c == self.nc - 1
        self.row_edge = jnp.logical_or(self.top, self.bottom)
        self.col_edge = jnp.logical_or(self.left, self.right)
        self.row_kind = jnp.where(self.top, 0, 1)
        self.col_kind = jnp.where(self.left, 0, 1)

    def at(self, f=None, r=None, c=None):
        return (
            self.f if f is None else f,
            self.r if r is None else r,
            self.c if c is None else c,
        )

    def row_group(self):
        other_r = self.nr - 1 - self.r
        other_c = self.nc - 1 - self.c
        return [
            (self.at(c=other_c), self.row_kind * 2 + 1, self.row_kind * 2 + 1),
            (self.at(r=other_r), self.row_kind * 2, (1 - self.row_kind) * 2),
            (self.at(r=other_r, c=other_c), self.row_kind * 2 + 1, (1 - self.row_kind) * 2 + 1),
        ]

    def col_group(self):
        other_r = self.nr - 1 - self.r
        other_c = self.nc - 1 - self.c
        return [
            (self.at(r=other_r), self.col_kind * 2 + 1, self.col_kind * 2 + 1),
            (self.at(c=other_c), self.col_kind * 2, (1 - self.col_kind) * 2),
            (self.at(r=other_r, c=other_c), self.col_kind * 2 + 1, (1 - self.col_kind) * 2 + 1),
        ]

    def ring(self, axis):
        index, count = {"face": (self.f, self.nf), "row": (self.r, self.nr), "col": (self.c, self.nc)}[axis]
        out = []
        for step in range(1, count):
            other = lax.rem(index + step, count)
            out.append((other, self.at(**{axis[0]: other}), step))
        return out


def start_group(group, src, slots, sems, back):
    for i, (device, slot, unused) in enumerate(group):
        send(src, slots.at[slot], sems.at[back, i], sems.at[back + 1, slot], device).start()


def wait_group(group, src, slots, sems, back):
    for i, (device, unused, slot) in enumerate(group):
        send(src, slots.at[slot], sems.at[back, i], sems.at[back + 1, slot], device).wait_recv()


def done_group(group, src, slots, sems, back):
    for i, (device, unused, slot) in enumerate(group):
        send(src, slots.at[slot], sems.at[back, i], sems.at[back + 1, slot], device).wait_send()


def start_ring(ring, me, src_of, slots, sems):
    for other, device, step in ring:
        send(src_of(other), slots.at[me], sems.at[0, step], sems.at[1, me], device).start()


def wait_ring(ring, src_of, slots, sems):
    for other, device, step in ring:
        send(src_of(other), slots.at[other], sems.at[0, step], sems.at[1, other], device).wait_recv()


def done_ring(ring, src_of, slots, sems):
    for other, device, step in ring:
        send(src_of(other), slots.at[other], sems.at[0, step], sems.at[1, other], device).wait_send()


def greet(barrier, device):
    pl.semaphore_signal(barrier, inc=1, device_id=device, device_id_type=MESH)


def oriented(strip, code, flip):
    turned = jnp.concatenate([strip[2:3], strip[1:2], strip[0:1]], axis=0)
    strip = jnp.where(code % 2 == 1, turned, strip)
    mirrored = dot(strip.reshape(RIM * CH, TC).astype(BF), flip).reshape(RIM, CH, TC)
    return jnp.where(code >= 2, mirrored, strip).astype(BF)


def step_kernel(
    dims,
    x_ref,
    prior_ref,
    cot_ref,
    kernel_ref,
    we_ref,
    wr_ref,
    wg_ref,
    wc_ref,
    sf,
    sc,
    next_out,
    prior_out,
    input_out,
    grads_out,
    natural,
    xw,
    strips,
    chosen,
    faces,
    pack,
    sides,
    col_strips,
    col_chosen,
    col_faces,
    spread,
    halo,
    xf,
    ef,
    shifted,
    taps,
    summed,
    back,
    prior,
    cot,
    total,
    edge_grad,
    ge,
    gr,
    gg,
    gc,
    grads,
    rim,
    edges,
    rim_sides,
    rim_faces,
    rim_chosen,
    rim_strips,
    row_sides,
    row_faces,
    row_chosen,
    row_strips,
    a1,
    a2_src,
    a2,
    a3_src,
    a3,
    a4_src,
    a4,
    a5_src,
    a5,
    near,
    group_sem,
    row_face_sem,
    col_face_sem,
    near_back,
    group_back,
    rim_face_sem,
    row_back_sem,
    s1,
    s2,
    s3,
    s4,
    s5,
):
    at = Place(dims)
    nf, nr, nc = dims
    part1 = PACK_ROWS // nf
    part2 = part1 // nc
    face_ring = at.ring("face")
    row_ring = at.ring("row")
    col_ring = at.ring("col")
    row_group = at.row_group()
    col_group = at.col_group()
    barrier = pltpu.get_barrier_semaphore()
    for ring in (face_ring, row_ring, col_ring):
        for unused, device, unused2 in ring:
            greet(barrier, device)
    corner = at.at(r=nr - 1 - at.r, c=nc - 1 - at.c)
    any_edge = jnp.logical_or(at.row_edge, at.col_edge)

    @pl.when(any_edge)
    def _():
        greet(barrier, corner)

    above = at.at(r=jnp.maximum(at.r - 1, 0))
    below = at.at(r=jnp.minimum(at.r + 1, nr - 1))
    before = at.at(c=jnp.maximum(at.c - 1, 0))
    after = at.at(c=jnp.minimum(at.c + 1, nc - 1))
    has_above = jnp.logical_not(at.top)
    has_below = jnp.logical_not(at.bottom)
    has_before = jnp.logical_not(at.left)
    has_after = jnp.logical_not(at.right)

    natural[...] = x_ref[...].astype(F32).reshape(CH * TR, TC)
    for y in range(TR):
        xw[RIM + y] = natural[pl.ds(y, CH, stride=TR), :].astype(BF)
    for row in range(PR):
        spread[:, row * TC : (row + 1) * TC] = spread_block(row)
    prior[...] = prior_ref[...].astype(F32).reshape(CH * TR, TC)
    cot[...] = cot_ref[...].astype(F32).reshape(CH * TR, TC)
    for ref in (ge, gr, gg, gc):
        ref[...] = jnp.zeros_like(ref)
    flip = flip_matrix()
    pl.semaphore_wait(barrier, nf + nr + nc - 3 + jnp.where(any_edge, 1, 0))

    def to_above():
        return send(xw.at[pl.ds(RIM, RIM)], xw.at[pl.ds(RIM + TR, RIM)], near.at[0, 0], near.at[1, 0], above)

    def to_below():
        return send(xw.at[pl.ds(TR, RIM)], xw.at[pl.ds(0, RIM)], near.at[0, 1], near.at[1, 1], below)

    def own_edge():
        return xw.at[pl.ds(jnp.where(at.top, RIM, TR), RIM)]

    @pl.when(at.row_edge)
    def _():
        start_group(row_group, own_edge(), strips, group_sem, 0)

    @pl.when(has_above)
    def _():
        to_above().start()

    @pl.when(has_below)
    def _():
        to_below().start()

    @pl.when(at.row_edge)
    def _():
        strips[at.row_kind * 2] = own_edge()[...]
        wait_group(row_group, own_edge(), strips, group_sem, 0)
        taker = partner_of(sf, at.row_kind, at.f, nf)
        code = sc[at.row_kind, taker]
        picked = strips[kind_of(at.row_kind, code) * 2 + code // 2]
        chosen[...] = picked
        start_ring(face_ring, at.f, lambda other: chosen, faces, row_face_sem)
        faces[at.f] = picked
        wait_ring(face_ring, lambda other: chosen, faces, row_face_sem)
        strip = oriented(faces[sf[at.row_kind, at.f]].astype(F32), sc[at.row_kind, at.f], flip)
        xw[pl.ds(jnp.where(at.top, 0, RIM + TR), RIM)] = strip

    @pl.when(has_below)
    def _():
        to_above().wait_recv()

    @pl.when(has_above)
    def _():
        to_below().wait_recv()

    flat = jnp.concatenate([xw[row] for row in range(PR)], axis=1)
    pack[...] = dot_nt(flat, spread[...]).astype(BF)

    def to_before():
        return send(pack, sides.at[1], near.at[0, 2], near.at[1, 2], before)

    def to_after():
        return send(pack, sides.at[0], near.at[0, 3], near.at[1, 3], after)

    @pl.when(at.col_edge)
    def _():
        start_group(col_group, pack, col_strips, group_sem, 2)

    @pl.when(has_before)
    def _():
        to_before().start()

    @pl.when(has_after)
    def _():
        to_after().start()

    xf[...] = xw[...].astype(F32)

    @pl.when(at.col_edge)
    def _():
        side = at.col_kind + 2
        col_strips[at.col_kind * 2] = pack[...]
        wait_group(col_group, pack, col_strips, group_sem, 2)
        code = sc[side, partner_of(sf, side, at.f, nf)]
        picked = col_strips[kind_of(at.col_kind, code) * 2 + code // 2]
        col_chosen[...] = picked
        start_ring(face_ring, at.f, lambda other: col_chosen, col_faces, col_face_sem)
        col_faces[at.f] = picked
        wait_ring(face_ring, lambda other: col_chosen, col_faces, col_face_sem)
        strip = col_faces[sf[side, at.f]]
        sides[at.col_kind] = dot(strip, turn_matrix(sc[side, at.f])).astype(BF)

    @pl.when(has_after)
    def _():
        to_before().wait_recv()

    @pl.when(has_before)
    def _():
        to_after().wait_recv()

    place = lax.broadcasted_iota(jnp.int32, (CH, TC), 1) % 8
    low = place < RIM
    halo[...] = jnp.where(low, sides[0].astype(F32), sides[1].astype(F32)).astype(BF)

    ends = dot(halo[...], spread[...])
    for row in range(PR):
        ef[row] = ends[:, row * TC : (row + 1) * TC]
    lane = lax.broadcasted_iota(jnp.int32, (PR, 8, TC), 2)
    lane2 = lax.broadcasted_iota(jnp.int32, (8, TC), 1)
    kernel_t = kernel_ref[...].T
    gc[:, 0 : KS * KS] = kernel_t

    def forward(g, carry):
        part = pl.ds(pl.multiple_of(g * 8, 8), 8)
        values = gc[part, :]
        sums = jnp.zeros((TR, 8, TC), F32)
        inside = xf[:, part, :]
        outside = ef[:, part, :]
        for b in range(KS):
            d = b - RIM
            rows = inside
            if d:
                wrapped = lane < d if d > 0 else lane >= TC + d
                rows = pltpu.roll(jnp.where(wrapped, outside, inside), (-d) % TC, 2)
            shifted[b, :, part, :] = rows
            for a in range(KS):
                tap = a * KS + b
                weight = jnp.broadcast_to(values[:, tap : tap + 1], (8, TC))
                taps[tap, part, :] = weight
                sums = sums + weight[None] * rows[a : a + TR]
        summed[:, part, :] = sums
        return carry

    lax.fori_loop(0, CH // 8, forward, 0)
    gc[...] = jnp.zeros_like(gc)

    we = we_ref[...]
    wr_t = wr_ref[...]
    wg = wg_ref[...]
    wc_t = wc_ref[...]
    we_t = we.T
    wr = wr_t.T
    wg_t = wg.T
    wc = wc_t.T

    def chunk(i, carry):
        r0 = i * 2

        def pair(load):
            return jnp.concatenate([load(r0), load(r0 + 1)], axis=1)

        s = pair(lambda y: summed[y])
        center = s - jnp.mean(s, axis=0, keepdims=True)
        scale = lax.rsqrt(jnp.mean(center * center, axis=0, keepdims=True) + 1e-06)
        unit = center * scale
        normed = unit.astype(BF)
        hidden = dot(we_t, normed)
        acts = []
        slopes = []
        for start in range(0, HID, 32):
            h = hidden[start : start + 32]
            cdf = 0.5 + 0.5 * lax.erf(h * math.sqrt(0.5))
            acts.append((h * cdf).astype(BF))
            slopes.append(cdf + h * (jnp.exp(-0.5 * h * h) * (1.0 / math.sqrt(2.0 * math.pi))))
        act = jnp.concatenate(acts, axis=0)
        slope = jnp.concatenate(slopes, axis=0)
        out = (pair(lambda y: xf[RIM + y]) + dot(wr_t, act)).astype(BF)
        earlier = pair(lambda y: prior[pl.ds(y, CH, stride=TR), :])
        joined = jnp.concatenate([out, earlier.astype(BF)], axis=0)
        gates = jax.nn.sigmoid(dot(wg_t, joined))
        update = gates[:CH]
        reset = gates[CH:]
        joined_reset = jnp.concatenate([out, (reset * earlier).astype(BF)], axis=0)
        proposal = jnp.tanh(dot(wc_t, joined_reset))
        result = (1.0 - update) * earlier + update * proposal
        g = pair(lambda y: cot[pl.ds(y, CH, stride=TR), :])
        d_cand = (g * update * (1.0 - proposal * proposal)).astype(BF)
        d_joined_reset = dot(wc, d_cand)
        d_reset = d_joined_reset[CH:]
        d_gates = jnp.concatenate(
            [
                g * (proposal - earlier) * (update * (1.0 - update)),
                d_reset * earlier * (reset * (1.0 - reset)),
            ],
            axis=0,
        ).astype(BF)
        d_joined = dot(wg, d_gates)
        d_out = (d_joined_reset[:CH] + d_joined[:CH]).astype(BF)
        d_prior = g * (1.0 - update) + d_reset * reset + d_joined[CH:]
        d_hidden = (dot(wr, d_out) * slope).astype(BF)
        d_normed = dot(we, d_hidden)
        ge[...] += dot_nt(normed, d_hidden)
        gr[...] += dot_nt(d_out, act)
        gg[...] += dot_nt(joined, d_gates)
        gc[...] += dot_nt(d_cand, joined_reset)
        d_summed = scale * (
            d_normed
            - jnp.mean(d_normed, axis=0, keepdims=True)
            - unit * jnp.mean(d_normed * unit, axis=0, keepdims=True)
        )
        d_center = d_out.astype(F32)
        for j in range(2):
            y = r0 + j
            cut = slice(j * TC, (j + 1) * TC)
            back[y] = d_summed[:, cut]
            total[RIM + y] = d_center[:, cut]
            next_out[y] = result[:, cut].astype(BF)
            prior_out[y] = d_prior[:, cut].astype(BF)
        return carry

    lax.fori_loop(0, TR // 2, chunk, 0)
    grads[0:64] = ge[:, :TC].astype(BF)
    grads[64:128] = ge[:, TC:].astype(BF)
    grads[128:192] = gr[:, :TC].astype(BF)
    grads[192:256] = gr[:, TC:].astype(BF)
    grads[256:384] = gg[...].astype(BF)
    grads[384:448] = gc[...].astype(BF)

    def piece1(other):
        return grads.at[pl.ds(pl.multiple_of(other * part1, part1), part1)]

    def start_shares(wanted):
        for other, device, step in face_ring:

            @pl.when((other == nf - 1) == wanted)
            def _(other=other, device=device, step=step):
                send(piece1(other), a1.at[at.f], s1.at[0, step], s1.at[1, at.f], device).start()

    start_shares(False)

    def backward_kernel(g, carry):
        part = pl.ds(pl.multiple_of(g * 8, 8), 8)
        rows = back[:, part, :]
        found = jnp.zeros((8, TC), F32)
        for b in range(KS):
            for a in range(KS):
                terms = jnp.sum(rows * shifted[b, a : a + TR, part, :], axis=0)
                found = jnp.where(lane2 == a * KS + b, jnp.sum(terms, axis=1, keepdims=True), found)
        gc[part, :] = found
        return carry

    lax.fori_loop(0, CH // 8, backward_kernel, 0)
    grads[448:512] = gc[...].astype(BF)
    start_shares(True)
    a1[at.f] = piece1(at.f)[...]

    def backward(g, carry):
        part = pl.ds(pl.multiple_of(g * 8, 8), 8)
        rows = back[:, part, :]
        inner = jnp.zeros((PR, 8, TC), F32)
        outer = jnp.zeros((PR, 8, TC), F32)
        for b in range(KS):
            d = b - RIM
            columns = [None] * PR
            for a in range(KS):
                product = taps[a * KS + b, part, :][None] * rows
                for y in range(TR):
                    columns[y + a] = product[y] if columns[y + a] is None else columns[y + a] + product[y]
            moved = jnp.stack(columns)
            if d == 0:
                inner = inner + moved
                continue
            moved = pltpu.roll(moved, d % TC, 2)
            wrapped = lane < d if d > 0 else lane >= TC + d
            inner = inner + jnp.where(wrapped, 0.0, moved)
            outer = outer + jnp.where(wrapped, moved, 0.0)
        total[0:RIM, part, :] = inner[0:RIM]
        total[RIM : RIM + TR, part, :] = total[RIM : RIM + TR, part, :] + inner[RIM : RIM + TR]
        total[RIM + TR :, part, :] = inner[RIM + TR :]
        edge_grad[:, part, :] = outer
        return carry

    lax.fori_loop(0, CH // 8, backward, 0)
    flat = jnp.concatenate([edge_grad[row] for row in range(PR)], axis=1).astype(BF)
    rim[...] = dot_nt(flat, spread[...]).astype(BF)

    def rim_before():
        return send(rim, rim_sides.at[1], near_back.at[0, 2], near_back.at[1, 2], before)

    def rim_after():
        return send(rim, rim_sides.at[0], near_back.at[0, 3], near_back.at[1, 3], after)

    @pl.when(at.col_edge)
    def _():
        start_ring(face_ring, at.f, lambda other: rim, rim_faces, rim_face_sem)

    @pl.when(has_before)
    def _():
        rim_before().start()

    @pl.when(has_after)
    def _():
        rim_after().start()

    wait_ring(face_ring, piece1, a1, s1)
    partial = a1[0].astype(F32)
    for other in range(1, nf):
        partial = partial + a1[other].astype(F32)
    a2_src[...] = partial

    def piece2(other):
        return a2_src.at[pl.ds(pl.multiple_of(other * part2, part2), part2)]

    start_ring(col_ring, at.c, piece2, a2, s2)
    a2[at.c] = piece2(at.c)[...]

    @pl.when(at.col_edge)
    def _():
        side = at.col_kind + 2
        rim_faces[at.f] = rim[...]
        wait_ring(face_ring, lambda other: rim, rim_faces, rim_face_sem)
        taker = partner_of(sf, side, at.f, nf)
        strip = rim_faces[taker].astype(F32)
        strip = jnp.where(low == at.left, strip, 0.0).astype(BF)
        turned = dot(strip, turn_matrix(sc[side, taker])).astype(BF)
        rim_chosen[...] = turned
        start_group(col_group, rim_chosen, rim_strips, group_back, 0)
        rim_strips[at.col_kind * 2] = turned

    wait_ring(col_ring, piece2, a2, s2)
    partial = a2[0]
    for other in range(1, nc):
        partial = partial + a2[other]
    a3_src[...] = partial
    start_ring(row_ring, at.r, lambda other: a3_src, a3, s3)
    a3[at.r] = partial

    def seam_total(slots, kind, first_side):
        gathered = None
        for side_bit in range(2):
            taker = partner_of(sf, first_side + side_bit, at.f, nf)
            code = sc[first_side + side_bit, taker]
            mine = kind_of(side_bit, code) == kind
            for mirror in range(2):
                use = jnp.logical_and(mine, code // 2 == mirror)
                term = jnp.where(use, slots[side_bit * 2 + mirror].astype(F32), 0.0)
                gathered = term if gathered is None else gathered + term
        return gathered

    @pl.when(at.col_edge)
    def _():
        wait_group(col_group, rim_chosen, rim_strips, group_back, 0)
        rim_sides[at.col_kind] = seam_total(rim_strips, at.col_kind, 2).astype(BF)

    @pl.when(has_after)
    def _():
        rim_before().wait_recv()

    @pl.when(has_before)
    def _():
        rim_after().wait_recv()

    returned = jnp.where(low, rim_sides[1].astype(F32), rim_sides[0].astype(F32)).astype(BF)
    ends = dot(returned, spread[...])
    for row in range(PR):
        total[row] = total[row] + ends[:, row * TC : (row + 1) * TC]
    edges[0] = total[0:RIM].astype(BF)
    edges[1] = total[RIM + TR : PR].astype(BF)

    def grad_above():
        return send(edges.at[0], row_sides.at[1], near_back.at[0, 0], near_back.at[1, 0], above)

    def grad_below():
        return send(edges.at[1], row_sides.at[0], near_back.at[0, 1], near_back.at[1, 1], below)

    def own_grad():
        return edges.at[at.row_kind]

    @pl.when(at.row_edge)
    def _():
        start_ring(face_ring, at.f, lambda other: own_grad(), row_faces, row_back_sem)

    @pl.when(has_above)
    def _():
        grad_above().start()

    @pl.when(has_below)
    def _():
        grad_below().start()

    wait_ring(row_ring, lambda other: a3_src, a3, s3)
    partial = a3[0]
    for other in range(1, nr):
        partial = partial + a3[other]
    a4_src[...] = partial
    start_ring(col_ring, at.c, lambda other: a4_src, a4, s4)
    a4[at.c] = partial

    @pl.when(at.row_edge)
    def _():
        row_faces[at.f] = own_grad()[...]
        wait_ring(face_ring, lambda other: own_grad(), row_faces, row_back_sem)
        taker = partner_of(sf, at.row_kind, at.f, nf)
        strip = oriented(row_faces[taker].astype(F32), sc[at.row_kind, taker], flip_matrix())
        row_chosen[...] = strip
        start_group(row_group, row_chosen, row_strips, group_back, 2)
        row_strips[at.row_kind * 2] = strip

    wait_ring(col_ring, lambda other: a4_src, a4, s4)
    full = jnp.concatenate([a4[other] for other in range(nc)], axis=0).astype(BF)
    a5_src[...] = full
    start_ring(face_ring, at.f, lambda other: a5_src, a5, s5)
    a5[at.f] = full

    @pl.when(has_below)
    def _():
        grad_above().wait_recv()
        total[TR : TR + RIM] = total[TR : TR + RIM] + row_sides[1].astype(F32)

    @pl.when(has_above)
    def _():
        grad_below().wait_recv()
        total[RIM : 2 * RIM] = total[RIM : 2 * RIM] + row_sides[0].astype(F32)

    @pl.when(at.row_edge)
    def _():
        wait_group(row_group, row_chosen, row_strips, group_back, 2)
        gathered = seam_total(row_strips, at.row_kind, 0)
        spot = pl.ds(jnp.where(at.top, RIM, TR), RIM)
        total[spot] = total[spot] + gathered

    input_out[...] = total[RIM : RIM + TR].astype(BF)
    wait_ring(face_ring, lambda other: a5_src, a5, s5)
    for other in range(nf):
        grads_out[other * part1 : (other + 1) * part1] = a5[other]

    @pl.when(has_above)
    def _():
        to_above().wait_send()
        grad_above().wait_send()

    @pl.when(has_below)
    def _():
        to_below().wait_send()
        grad_below().wait_send()

    @pl.when(has_before)
    def _():
        to_before().wait_send()
        rim_before().wait_send()

    @pl.when(has_after)
    def _():
        to_after().wait_send()
        rim_after().wait_send()

    @pl.when(at.row_edge)
    def _():
        done_group(row_group, own_edge(), strips, group_sem, 0)
        done_ring(face_ring, lambda other: chosen, faces, row_face_sem)
        done_ring(face_ring, lambda other: own_grad(), row_faces, row_back_sem)
        done_group(row_group, row_chosen, row_strips, group_back, 2)

    @pl.when(at.col_edge)
    def _():
        done_group(col_group, pack, col_strips, group_sem, 2)
        done_ring(face_ring, lambda other: col_chosen, col_faces, col_face_sem)
        done_ring(face_ring, lambda other: rim, rim_faces, rim_face_sem)
        done_group(col_group, rim_chosen, rim_strips, group_back, 0)

    done_ring(face_ring, piece1, a1, s1)
    done_ring(col_ring, piece2, a2, s2)
    done_ring(row_ring, lambda other: a3_src, a3, s3)
    done_ring(col_ring, lambda other: a4_src, a4, s4)
    done_ring(face_ring, lambda other: a5_src, a5, s5)


def finish_kernel(
    grad_scale,
    next_rows,
    prior_rows,
    input_rows,
    grads,
    next_out,
    input_out,
    prior_out,
    kernel_out,
    expand_out,
    reduce_out,
    gates_out,
    candidate_out,
    natural,
):
    for rows, out in ((next_rows, next_out), (input_rows, input_out), (prior_rows, prior_out)):
        for y in range(TR):
            natural[pl.ds(y, CH, stride=TR), :] = rows[y].astype(F32)
        out[...] = natural[...].reshape(CH, TR, TC).astype(BF)
    scaled = grads[...].astype(F32) * grad_scale
    expand_out[:, :TC] = scaled[0:64]
    expand_out[:, TC:] = scaled[64:128]
    reduce_out[:, :TC] = scaled[128:192]
    reduce_out[:, TC:] = scaled[192:256]
    gates_out[...] = scaled[256:384]
    candidate_out[...] = scaled[384:448]
    kernel_out[...] = scaled[448:512].T[: KS * KS]


def dma(*shape):
    return pltpu.SemaphoreType.DMA(shape)


def whole_step(dims, x, prior, cot, kernel_t, we, wr_t, wg, wc_t, sf, sc):
    nf, nr, nc = dims
    part1 = PACK_ROWS // nf
    part2 = part1 // nc
    wide = (PR, CH, TC)
    tile = (TR, CH, TC)
    strip = (RIM, CH, TC)
    flat = (CH * TR, TC)
    edge = (CH, TC)
    rows = jax.ShapeDtypeStruct(tile, BF)
    bf16_scratch = [
        wide,
        (4,) + strip,
        strip,
        (nf,) + strip,
        edge,
        (2,) + edge,
        (4,) + edge,
        edge,
        (nf,) + edge,
        (TC, PR * TC),
        edge,
    ]
    f32_scratch = [
        wide,
        wide,
        (KS,) + wide,
        (KS * KS, CH, TC),
        tile,
        tile,
        flat,
        flat,
        wide,
        wide,
        (CH, HID),
        (CH, HID),
        (2 * CH, 2 * CH),
        (CH, 2 * CH),
    ]
    back_scratch = [
        (PACK_ROWS, TC),
        edge,
        (2,) + strip,
        (2,) + edge,
        (nf,) + edge,
        edge,
        (4,) + edge,
        (2,) + strip,
        (nf,) + strip,
        strip,
        (4,) + strip,
        (nf, part1, TC),
    ]
    sum_scratch = [(part1, TC), (nc, part2, TC), (part2, TC), (nr, part2, TC), (part2, TC), (nc, part2, TC)]
    return pl.pallas_call(
        functools.partial(step_kernel, dims),
        out_shape=(rows, rows, rows, jax.ShapeDtypeStruct((PACK_ROWS, TC), BF)),
        in_specs=[VMEM] * 8 + [SMEM] * 2,
        out_specs=(VMEM,) * 4,
        scratch_shapes=[pltpu.VMEM(flat, F32)]
        + [pltpu.VMEM(shape, BF) for shape in bf16_scratch]
        + [pltpu.VMEM(shape, F32) for shape in f32_scratch]
        + [pltpu.VMEM(shape, BF) for shape in back_scratch]
        + [pltpu.VMEM(shape, F32) for shape in sum_scratch]
        + [pltpu.VMEM((part1, TC), BF), pltpu.VMEM((nf, part1, TC), BF)]
        + [dma(2, 4), dma(4, 4), dma(2, nf), dma(2, nf)]
        + [dma(2, 4), dma(4, 4), dma(2, nf), dma(2, nf)]
        + [dma(2, nf), dma(2, nc), dma(2, nr), dma(2, nc), dma(2, nf)],
        compiler_params=pltpu.CompilerParams(
            collective_id=0, has_side_effects=True, vmem_limit_bytes=LIMIT
        ),
        name="whole_step",
    )(x, prior, cot, kernel_t, we, wr_t, wg, wc_t, sf, sc)


def finish(grad_scale, next_rows, prior_rows, input_rows, grads):
    tile = jax.ShapeDtypeStruct((CH, TR, TC), BF)
    shapes = ((KS * KS, CH), (CH, HID), (CH, HID), (2 * CH, 2 * CH), (CH, 2 * CH))
    return pl.pallas_call(
        functools.partial(finish_kernel, grad_scale),
        out_shape=(tile,) * 3 + tuple(jax.ShapeDtypeStruct(shape, F32) for shape in shapes),
        in_specs=[VMEM] * 4,
        out_specs=(VMEM,) * 8,
        scratch_shapes=[pltpu.VMEM((CH * TR, TC), F32)],
        compiler_params=pltpu.CompilerParams(vmem_limit_bytes=LIMIT),
        name="finish",
    )(next_rows, prior_rows, input_rows, grads)


def body(dims, cell_total, block_in, hidden_state, state_cotangent, kernel, we, wr, wg, wc, sf, sc):
    rows = whole_step(
        dims, block_in[0], hidden_state[0], state_cotangent[0], kernel.T, we, wr.T, wg, wc.T, sf.T, sc.T
    )
    done = finish(1.0 / math.sqrt(cell_total), *rows)
    return (
        done[0][None],
        done[1][None],
        done[2][None],
        done[3].T,
        done[4],
        done[5].T,
        done[6],
        done[7].T,
    )


def solution(mesh):
    dims = tuple(mesh.shape[name] for name in AXES)
    cell_total = dims[0] * dims[1] * dims[2] * TR * TC
    tiles = P("face", None, "row", "col")
    return jax.shard_map(
        functools.partial(body, dims, cell_total),
        mesh=mesh,
        in_specs=(tiles,) * 3 + (P(),) * 7,
        out_specs=(tiles,) * 3 + (P(),) * 5,
        check_vma=False,
    )
```

time: 102 us -> 88 us (0.86)
  the two profiles are of different devices: /device:TPU:2 before, /device:TPU:70 now
where the time goes in v2:
time: 88 us; the launch traced here: 87.5 us
  Pallas kernels  79.7 us (91%)
  local copies, waits for them, and re-layouts  7.13 us (8%)
    pallas_call x1, Pallas kernels, whole_step(): pl.pallas_call(functools.partial(step_kernel, dims), out_shape=(rows, row...  78.7 us
    unnamed x20, local copies, waits for them, and re-layouts  7.13 us

profile of v2, /device:TPU:70, one launch (start us, length us, event | category | flops | bytes accessed | tf_op | source)
XLA Modules:
  0.0 87.5 jit_solution(14781438664285065498)
XLA Ops:
  0.6 0.0 copy-start.9
  0.6 0.0 copy-start.8
  0.7 0.7 copy-done.9
  1.3 0.0 copy-done.8
  1.3 0.0 copy-start
  1.3 0.9 %copy-done = bf16[1,64,8,128]{3,2,1,0:T(8,128)(2,1)S(1)} copy-done((bf16[1,64,8,128]{3,2,1,0:T(8,128)(2,1)S(1)}, bf16[1,64,8,128]{3,2,1,0:T(8,128)(2,1)}, u32[]{:S(2)}) %copy-start) | copy-done | bytes 131096
  2.2 0.0 copy-start.1
  2.2 0.9 %copy-done.1 = bf16[1,64,8,128]{3,2,1,0:T(8,128)(2,1)S(1)} copy-done((bf16[1,64,8,128]{3,2,1,0:T(8,128)(2,1)S(1)}, bf16[1,64,8,128]{3,2,1,0:T(8,128)(2,1)}, u32[]{:S(2)}) %copy-start.1) | copy-done | bytes 131096
  3.1 0.0 copy-start.2
  3.1 0.9 %copy-done.2 = bf16[1,64,8,128]{3,2,1,0:T(8,128)(2,1)S(1)} copy-done((bf16[1,64,8,128]{3,2,1,0:T(8,128)(2,1)S(1)}, bf16[1,64,8,128]{3,2,1,0:T(8,128)(2,1)}, u32[]{:S(2)}) %copy-start.2) | copy-done | bytes 131096
  4.0 0.0 copy-start.3
  4.1 0.8 copy-done.3
  4.8 0.0 copy-start.4
  4.8 0.8 copy-done.4
  5.6 0.0 copy-start.5
  5.6 0.8 copy-done.5
  6.3 0.0 copy-start.6
  6.3 0.7 copy-done.6
  7.1 0.0 copy-start.7
  7.1 0.7 copy-done.7
  7.8 78.7 %whole_step.1 = (bf16[8,64,128]{2,1,0:T(8,128)(2,1)S(1)}, bf16[8,64,128]{2,1,0:T(8,128)(2,1)S(1)}, bf16[8,64,128]{2,1,0:T(8,128)(2,1)S(1)}, bf16[512,128]{1,0:T(8,128)(2,1)S(1)}) custom-call(bf16[64,8,128]{2,1,0:T(8,128)(2,1)S(1)} %bitcast.14, bf16[64,8,128]{2,1,0:T(8,128)(2,1)S(1)} %bitcast.15, bf16[64,8,128]{2,1,0:T(8,128)(2,1)S(1)} %bitcast.16, ...), custom_call_target="tpu_custom_call" | custom-call | tf_op jit(solution)/shard_map/whole_step/pallas_call | solution.py:833
  86.5 0.9 %finish.1 = (bf16[64,8,128]{2,1,0:T(8,128)(2,1)}, bf16[64,8,128]{2,1,0:T(8,128)(2,1)}, bf16[64,8,128]{2,1,0:T(8,128)(2,1)}, f32[49,64]{1,0:T(8,128)}, f32[64,256...) custom-call(bf16[8,64,128]{2,1,0:T(8,128)(2,1)S(1)} %get-tuple-element.20.next_rows, ...), custom_call_target="tpu_custom_call" | custom-call | tf_op jit(solution)/shard_map/finish/pallas_call | solution.py:857
Async XLA Ops:
  0.6 0.7 copy-start.9
  0.6 0.7 copy-start.8
  1.3 0.9 %copy-start = (bf16[1,64,8,128]{3,2,1,0:T(8,128)(2,1)S(1)}, bf16[1,64,8,128]{3,2,1,0:T(8,128)(2,1)}, u32[]{:S(2)}) copy-start(bf16[1,64,8,128]{3,2,1,0:T(8,128)(2,1)} %param.10) | copy-start | bytes 393220
  2.2 0.9 %copy-start.1 = (bf16[1,64,8,128]{3,2,1,0:T(8,128)(2,1)S(1)}, bf16[1,64,8,128]{3,2,1,0:T(8,128)(2,1)}, u32[]{:S(2)}) copy-start(bf16[1,64,8,128]{3,2,1,0:T(8,128)(2,1)} %param.11) | copy-start | bytes 393220
  3.1 0.9 %copy-start.2 = (bf16[1,64,8,128]{3,2,1,0:T(8,128)(2,1)S(1)}, bf16[1,64,8,128]{3,2,1,0:T(8,128)(2,1)}, u32[]{:S(2)}) copy-start(bf16[1,64,8,128]{3,2,1,0:T(8,128)(2,1)} %param.12) | copy-start | bytes 393220
  4.0 0.8 copy-start.3
  4.8 0.8 copy-start.4
  5.6 0.8 copy-start.5
  6.3 0.7 copy-start.6
  7.1 0.7 copy-start.7

commit v3 on v2

--- a/solution.py
+++ b/solution.py
@@ -21,8 +21,8 @@
 F32 = jnp.float32
 MESH = pl.DeviceIdType.MESH
 VMEM = pl.BlockSpec(memory_space=pltpu.VMEM)
-SMEM = pl.BlockSpec(memory_space=pltpu.SMEM)
-LIMIT = 40 * 1024 * 1024
+HBM = pl.BlockSpec(memory_space=pltpu.HBM)
+LIMIT = 60 * 1024 * 1024
 
 
 def spread_block(row):
@@ -78,6 +78,38 @@
 def kind_of(side_bit, code):
     odd = lax.rem(code, 2)
     return jnp.where(side_bit == 0, 1 - odd, odd)
+
+
+def corner_of(sf, sc, face, v, h):
+    beside = sf[h + 2, face]
+    code = sc[h + 2, face]
+    reverse = code // 2
+    v_there = (v + reverse) % 2
+    owner = sf[v_there, beside]
+    code_there = sc[v_there, beside]
+    reverse_there = code_there // 2
+    block = kind_of(v_there, code_there) * 2 + (kind_of(h, code) + reverse_there) % 2
+    return owner, block, (code_there + reverse) % 2, (code + reverse_there) % 2
+
+
+def corner_lanes(lane, v, h, block, row_turn, col_turn):
+    i = lane // 8 - jnp.where(v == 0, 0, RIM + TR)
+    j = lane % 8 - jnp.where(h == 0, 0, RIM)
+    inside = jnp.logical_and(
+        jnp.logical_and(i >= 0, i < RIM), jnp.logical_and(j >= 0, j < RIM)
+    )
+    i = jnp.where(row_turn == 1, RIM - 1 - i, i)
+    j = jnp.where(col_turn == 1, RIM - 1 - j, j)
+    return jnp.where(inside, block * 32 + i * 8 + j, -1)
+
+
+def one_hot(hit):
+    return jnp.where(hit, 1.0, 0.0).astype(BF)
+
+
+def block_lanes(lane, block, i):
+    mine = jnp.logical_and(lane // 8 == block * 4 + i, lane % 8 < RIM)
+    return jnp.where(mine, lane % 8 + jnp.where(block % 2 == 0, 0, TC - RIM), -1)
 
 
 class Place:
@@ -172,6 +204,20 @@
 
 def step_kernel(
     dims,
+    x_in,
+    prior_in,
+    cot_in,
+    kernel_in,
+    we_in,
+    wr_in,
+    wg_in,
+    wc_in,
+    sf_in,
+    sc_in,
+    next_out,
+    prior_out,
+    input_out,
+    grads_out,
     x_ref,
     prior_ref,
     cot_ref,
@@ -182,10 +228,15 @@
     wc_ref,
     sf,
     sc,
-    next_out,
-    prior_out,
-    input_out,
-    grads_out,
+    in_sem,
+    sides_late,
+    corner_pack,
+    corner_faces,
+    corner_out,
+    corner_strips,
+    corner_face_sem,
+    corner_group_sem,
+    pack_late,
     natural,
     xw,
     strips,
@@ -233,6 +284,7 @@
     a5_src,
     a5,
     near,
+    near_late,
     group_sem,
     row_face_sem,
     col_face_sem,
@@ -246,6 +298,16 @@
     s4,
     s5,
 ):
+    held = (x_ref, prior_ref, cot_ref, kernel_ref, we_ref, wr_ref, wg_ref, wc_ref, sf, sc)
+    given = (x_in, prior_in, cot_in, kernel_in, we_in, wr_in, wg_in, wc_in, sf_in, sc_in)
+    loads = [
+        pltpu.make_async_copy(source, target, in_sem.at[i])
+        for i, (source, target) in enumerate(zip(given, held))
+    ]
+    for load in loads:
+        load.start()
+    for ref in (sides, sides_late, rim_sides):
+        ref[...] = jnp.zeros_like(ref)
     at = Place(dims)
     nf, nr, nc = dims
     part1 = PACK_ROWS // nf
@@ -275,16 +337,28 @@
     has_before = jnp.logical_not(at.left)
     has_after = jnp.logical_not(at.right)
 
+    for row in range(PR):
+        spread[:, row * TC : (row + 1) * TC] = spread_block(row)
+    for ref in (ge, gr, gg, gc):
+        ref[...] = jnp.zeros_like(ref)
+    flip = flip_matrix()
+    edge_rows = jnp.zeros((RIM, CH, TC), BF)
+
+    @pl.when(at.top)
+    def _():
+        xw[0:RIM] = edge_rows
+
+    @pl.when(at.bottom)
+    def _():
+        xw[RIM + TR : PR] = edge_rows
+
+    for load in loads:
+        load.wait()
     natural[...] = x_ref[...].astype(F32).reshape(CH * TR, TC)
     for y in range(TR):
         xw[RIM + y] = natural[pl.ds(y, CH, stride=TR), :].astype(BF)
-    for row in range(PR):
-        spread[:, row * TC : (row + 1) * TC] = spread_block(row)
     prior[...] = prior_ref[...].astype(F32).reshape(CH * TR, TC)
     cot[...] = cot_ref[...].astype(F32).reshape(CH * TR, TC)
-    for ref in (ge, gr, gg, gc):
-        ref[...] = jnp.zeros_like(ref)
-    flip = flip_matrix()
     pl.semaphore_wait(barrier, nf + nr + nc - 3 + jnp.where(any_edge, 1, 0))
 
     def to_above():
@@ -307,6 +381,37 @@
     @pl.when(has_below)
     def _():
         to_below().start()
+
+    is_corner = jnp.logical_and(at.row_edge, at.col_edge)
+
+    @pl.when(has_below)
+    def _():
+        to_above().wait_recv()
+
+    @pl.when(has_above)
+    def _():
+        to_below().wait_recv()
+
+    flat = jnp.concatenate([xw[row] for row in range(PR)], axis=1)
+    pack[...] = dot_nt(flat, spread[...]).astype(BF)
+
+    def to_before():
+        return send(pack, sides.at[1], near.at[0, 2], near.at[1, 2], before)
+
+    def to_after():
+        return send(pack, sides.at[0], near.at[0, 3], near.at[1, 3], after)
+
+    @pl.when(at.col_edge)
+    def _():
+        start_group(col_group, pack, col_strips, group_sem, 2)
+
+    @pl.when(has_before)
+    def _():
+        to_before().start()
+
+    @pl.when(has_after)
+    def _():
+        to_after().start()
 
     @pl.when(at.row_edge)
     def _():
@@ -318,40 +423,19 @@
         chosen[...] = picked
         start_ring(face_ring, at.f, lambda other: chosen, faces, row_face_sem)
         faces[at.f] = picked
-        wait_ring(face_ring, lambda other: chosen, faces, row_face_sem)
-        strip = oriented(faces[sf[at.row_kind, at.f]].astype(F32), sc[at.row_kind, at.f], flip)
-        xw[pl.ds(jnp.where(at.top, 0, RIM + TR), RIM)] = strip
-
-    @pl.when(has_below)
-    def _():
-        to_above().wait_recv()
-
-    @pl.when(has_above)
-    def _():
-        to_below().wait_recv()
-
-    flat = jnp.concatenate([xw[row] for row in range(PR)], axis=1)
-    pack[...] = dot_nt(flat, spread[...]).astype(BF)
-
-    def to_before():
-        return send(pack, sides.at[1], near.at[0, 2], near.at[1, 2], before)
-
-    def to_after():
-        return send(pack, sides.at[0], near.at[0, 3], near.at[1, 3], after)
-
-    @pl.when(at.col_edge)
-    def _():
-        start_group(col_group, pack, col_strips, group_sem, 2)
-
-    @pl.when(has_before)
-    def _():
-        to_before().start()
-
-    @pl.when(has_after)
-    def _():
-        to_after().start()
-
-    xf[...] = xw[...].astype(F32)
+
+    @pl.when(is_corner)
+    def _():
+        source = lax.broadcasted_iota(jnp.int32, (TC, TC), 0)
+        lanes = lax.broadcasted_iota(jnp.int32, (TC, TC), 1)
+        blocks = jnp.zeros((CH, TC), F32)
+        for slot in range(4):
+            block = (slot // 2) * 2 + (at.col_kind + slot) % 2
+            for i in range(RIM):
+                blocks = blocks + dot(strips[slot, i], one_hot(block_lanes(lanes, block, i) == source))
+        corner_pack[...] = blocks.astype(BF)
+        start_ring(face_ring, at.f, lambda other: corner_pack, corner_faces, corner_face_sem)
+        corner_faces[at.f] = blocks.astype(BF)
 
     @pl.when(at.col_edge)
     def _():
@@ -363,10 +447,56 @@
         col_chosen[...] = picked
         start_ring(face_ring, at.f, lambda other: col_chosen, col_faces, col_face_sem)
         col_faces[at.f] = picked
+
+    def late_before():
+        return send(pack_late, sides_late.at[1], near_late.at[0, 0], near_late.at[1, 0], before)
+
+    def late_after():
+        return send(pack_late, sides_late.at[0], near_late.at[0, 1], near_late.at[1, 1], after)
+
+    @pl.when(at.row_edge)
+    def _():
+        wait_ring(face_ring, lambda other: chosen, faces, row_face_sem)
+        strip = oriented(faces[sf[at.row_kind, at.f]].astype(F32), sc[at.row_kind, at.f], flip)
+        xw[pl.ds(jnp.where(at.top, 0, RIM + TR), RIM)] = strip
+        late = jnp.zeros((CH, TC), F32)
+        source = lax.broadcasted_iota(jnp.int32, (TC, TC), 0)
+        lanes = lax.broadcasted_iota(jnp.int32, (TC, TC), 1)
+        first = jnp.where(at.top, 0, RIM + TR)
+        for i in range(RIM):
+            wanted = jnp.where(lanes % 8 < RIM, lanes % 8 + TC - RIM, lanes % 8 - RIM)
+            wanted = jnp.where(
+                jnp.logical_and(lanes // 8 == first + i, lanes % 8 < 2 * RIM), wanted, -1
+            )
+            late = late + dot(strip[i], one_hot(wanted == source))
+        pack_late[...] = late.astype(BF)
+
+        @pl.when(has_before)
+        def _():
+            late_before().start()
+
+        @pl.when(has_after)
+        def _():
+            late_after().start()
+
+    xf[...] = xw[...].astype(F32)
+
+    @pl.when(at.col_edge)
+    def _():
+        side = at.col_kind + 2
         wait_ring(face_ring, lambda other: col_chosen, col_faces, col_face_sem)
         strip = col_faces[sf[side, at.f]]
         sides[at.col_kind] = dot(strip, turn_matrix(sc[side, at.f])).astype(BF)
 
+    @pl.when(is_corner)
+    def _():
+        wait_ring(face_ring, lambda other: corner_pack, corner_faces, corner_face_sem)
+        source = lax.broadcasted_iota(jnp.int32, (TC, TC), 0)
+        lanes = lax.broadcasted_iota(jnp.int32, (TC, TC), 1)
+        owner, block, row_turn, col_turn = corner_of(sf, sc, at.f, at.row_kind, at.col_kind)
+        pick = one_hot(corner_lanes(lanes, at.row_kind, at.col_kind, block, row_turn, col_turn) == source)
+        sides_late[at.col_kind] = dot(corner_faces[owner], pick).astype(BF)
+
     @pl.when(has_after)
     def _():
         to_before().wait_recv()
@@ -374,10 +504,23 @@
     @pl.when(has_before)
     def _():
         to_after().wait_recv()
+
+    @pl.when(at.row_edge)
+    def _():
+        @pl.when(has_after)
+        def _():
+            late_before().wait_recv()
+
+        @pl.when(has_before)
+        def _():
+            late_after().wait_recv()
 
     place = lax.broadcasted_iota(jnp.int32, (CH, TC), 1) % 8
     low = place < RIM
-    halo[...] = jnp.where(low, sides[0].astype(F32), sides[1].astype(F32)).astype(BF)
+    halo[...] = (
+        jnp.where(low, sides[0].astype(F32), sides[1].astype(F32))
+        + jnp.where(low, sides_late[0].astype(F32), sides_late[1].astype(F32))
+    ).astype(BF)
 
     ends = dot(halo[...], spread[...])
     for row in range(PR):
@@ -581,6 +724,29 @@
     start_ring(col_ring, at.c, piece2, a2, s2)
     a2[at.c] = piece2(at.c)[...]
 
+    @pl.when(has_after)
+    def _():
+        rim_before().wait_recv()
+
+    @pl.when(has_before)
+    def _():
+        rim_after().wait_recv()
+
+    def add_columns(packed):
+        ends = dot(packed, spread[...])
+        for row in range(PR):
+            total[row] = total[row] + ends[:, row * TC : (row + 1) * TC]
+
+    add_columns(jnp.where(low, rim_sides[1].astype(F32), rim_sides[0].astype(F32)).astype(BF))
+
+    def own_grad():
+        return edges.at[at.row_kind]
+
+    @pl.when(at.row_edge)
+    def _():
+        edges[at.row_kind] = total[pl.ds(jnp.where(at.top, 0, RIM + TR), RIM)].astype(BF)
+        start_ring(face_ring, at.f, lambda other: own_grad(), row_faces, row_back_sem)
+
     @pl.when(at.col_edge)
     def _():
         side = at.col_kind + 2
@@ -588,11 +754,30 @@
         wait_ring(face_ring, lambda other: rim, rim_faces, rim_face_sem)
         taker = partner_of(sf, side, at.f, nf)
         strip = rim_faces[taker].astype(F32)
-        strip = jnp.where(low == at.left, strip, 0.0).astype(BF)
+        row = lax.broadcasted_iota(jnp.int32, (CH, TC), 1) // 8
+        beyond = jnp.logical_or(
+            jnp.logical_and(at.top, row < RIM), jnp.logical_and(at.bottom, row >= RIM + TR)
+        )
+        keep = jnp.logical_and(low == at.left, jnp.logical_not(beyond))
+        strip = jnp.where(keep, strip, 0.0).astype(BF)
         turned = dot(strip, turn_matrix(sc[side, taker])).astype(BF)
         rim_chosen[...] = turned
         start_group(col_group, rim_chosen, rim_strips, group_back, 0)
         rim_strips[at.col_kind * 2] = turned
+
+    @pl.when(is_corner)
+    def _():
+        source = lax.broadcasted_iota(jnp.int32, (TC, TC), 0)
+        lanes = lax.broadcasted_iota(jnp.int32, (TC, TC), 1)
+        blocks = jnp.zeros((CH, TC), F32)
+        for other in range(nf):
+            owner, block, row_turn, col_turn = corner_of(sf, sc, other, at.row_kind, at.col_kind)
+            wanted = corner_lanes(source, at.row_kind, at.col_kind, block, row_turn, col_turn)
+            wanted = jnp.where(owner == at.f, wanted, -1)
+            blocks = blocks + dot(rim_faces[other], one_hot(wanted == lanes))
+        corner_out[...] = blocks.astype(BF)
+        start_group(row_group, corner_out, corner_strips, corner_group_sem, 0)
+        corner_strips[at.row_kind * 2] = blocks.astype(BF)
 
     wait_ring(col_ring, piece2, a2, s2)
     partial = a2[0]
@@ -617,22 +802,8 @@
     @pl.when(at.col_edge)
     def _():
         wait_group(col_group, rim_chosen, rim_strips, group_back, 0)
-        rim_sides[at.col_kind] = seam_total(rim_strips, at.col_kind, 2).astype(BF)
-
-    @pl.when(has_after)
-    def _():
-        rim_before().wait_recv()
-
-    @pl.when(has_before)
-    def _():
-        rim_after().wait_recv()
-
-    returned = jnp.where(low, rim_sides[1].astype(F32), rim_sides[0].astype(F32)).astype(BF)
-    ends = dot(returned, spread[...])
-    for row in range(PR):
-        total[row] = total[row] + ends[:, row * TC : (row + 1) * TC]
-    edges[0] = total[0:RIM].astype(BF)
-    edges[1] = total[RIM + TR : PR].astype(BF)
+        back_rim = seam_total(rim_strips, at.col_kind, 2)
+        add_columns(jnp.where(low == at.left, 0.0, back_rim).astype(BF))
 
     def grad_above():
         return send(edges.at[0], row_sides.at[1], near_back.at[0, 0], near_back.at[1, 0], above)
@@ -640,19 +811,14 @@
     def grad_below():
         return send(edges.at[1], row_sides.at[0], near_back.at[0, 1], near_back.at[1, 1], below)
 
-    def own_grad():
-        return edges.at[at.row_kind]
-
-    @pl.when(at.row_edge)
-    def _():
-        start_ring(face_ring, at.f, lambda other: own_grad(), row_faces, row_back_sem)
-
     @pl.when(has_above)
     def _():
+        edges[0] = total[0:RIM].astype(BF)
         grad_above().start()
 
     @pl.when(has_below)
     def _():
+        edges[1] = total[RIM + TR : PR].astype(BF)
         grad_below().start()
 
     wait_ring(row_ring, lambda other: a3_src, a3, s3)
@@ -696,6 +862,19 @@
         spot = pl.ds(jnp.where(at.top, RIM, TR), RIM)
         total[spot] = total[spot] + gathered
 
+    @pl.when(is_corner)
+    def _():
+        wait_group(row_group, corner_out, corner_strips, corner_group_sem, 0)
+        blocks = corner_strips[0].astype(F32)
+        for slot in range(1, 4):
+            blocks = blocks + corner_strips[slot].astype(F32)
+        source = lax.broadcasted_iota(jnp.int32, (TC, TC), 0)
+        lanes = lax.broadcasted_iota(jnp.int32, (TC, TC), 1)
+        first = jnp.where(at.top, RIM, TR)
+        for i in range(RIM):
+            wanted = block_lanes(source, at.row_kind * 2 + at.col_kind, i)
+            total[first + i] = total[first + i] + dot(blocks.astype(BF), one_hot(wanted == lanes))
+
     input_out[...] = total[RIM : RIM + TR].astype(BF)
     wait_ring(face_ring, lambda other: a5_src, a5, s5)
     for other in range(nf):
@@ -727,6 +906,19 @@
         done_ring(face_ring, lambda other: chosen, faces, row_face_sem)
         done_ring(face_ring, lambda other: own_grad(), row_faces, row_back_sem)
         done_group(row_group, row_chosen, row_strips, group_back, 2)
+
+        @pl.when(has_before)
+        def _():
+            late_before().wait_send()
+
+        @pl.when(has_after)
+        def _():
+            late_after().wait_send()
+
+    @pl.when(is_corner)
+    def _():
+        done_ring(face_ring, lambda other: corner_pack, corner_faces, corner_face_sem)
+        done_group(row_group, corner_out, corner_strips, corner_group_sem, 0)
 
     @pl.when(at.col_edge)
     def _():
@@ -776,7 +968,7 @@
     return pltpu.SemaphoreType.DMA(shape)
 
 
-def whole_step(dims, x, prior, cot, kernel_t, we, wr_t, wg, wc_t, sf, sc):
+def whole_step(dims, *given):
     nf, nr, nc = dims
     part1 = PACK_ROWS // nf
     part2 = part1 // nc
@@ -833,22 +1025,27 @@
     return pl.pallas_call(
         functools.partial(step_kernel, dims),
         out_shape=(rows, rows, rows, jax.ShapeDtypeStruct((PACK_ROWS, TC), BF)),
-        in_specs=[VMEM] * 8 + [SMEM] * 2,
+        in_specs=[HBM] * 10,
         out_specs=(VMEM,) * 4,
-        scratch_shapes=[pltpu.VMEM(flat, F32)]
+        scratch_shapes=[pltpu.VMEM(value.shape, value.dtype) for value in given[:8]]
+        + [pltpu.SMEM(value.shape, value.dtype) for value in given[8:]]
+        + [dma(10)]
+        + [pltpu.VMEM((2,) + edge, BF), pltpu.VMEM(edge, BF), pltpu.VMEM((nf,) + edge, BF)]
+        + [pltpu.VMEM(edge, BF), pltpu.VMEM((4,) + edge, BF), dma(2, nf), dma(2, 4), pltpu.VMEM(edge, BF)]
+        + [pltpu.VMEM(flat, F32)]
         + [pltpu.VMEM(shape, BF) for shape in bf16_scratch]
         + [pltpu.VMEM(shape, F32) for shape in f32_scratch]
         + [pltpu.VMEM(shape, BF) for shape in back_scratch]
         + [pltpu.VMEM(shape, F32) for shape in sum_scratch]
         + [pltpu.VMEM((part1, TC), BF), pltpu.VMEM((nf, part1, TC), BF)]
-        + [dma(2, 4), dma(4, 4), dma(2, nf), dma(2, nf)]
+        + [dma(2, 4), dma(2, 2), dma(4, 4), dma(2, nf), dma(2, nf)]
         + [dma(2, 4), dma(4, 4), dma(2, nf), dma(2, nf)]
         + [dma(2, nf), dma(2, nc), dma(2, nr), dma(2, nc), dma(2, nf)],
         compiler_params=pltpu.CompilerParams(
             collective_id=0, has_side_effects=True, vmem_limit_bytes=LIMIT
         ),
         name="whole_step",
-    )(x, prior, cot, kernel_t, we, wr_t, wg, wc_t, sf, sc)
+    )(*given)
 
 
 def finish(grad_scale, next_rows, prior_rows, input_rows, grads):

time: 88 us -> 70.6 us (0.80)
  the two profiles are of different devices: /device:TPU:70 before, /device:TPU:1 now
where the time goes in v3:
time: 70.6 us; the launch traced here: 69.4 us
  Pallas kernels  68.7 us (97%)
    pallas_call x1, Pallas kernels, whole_step(): pl.pallas_call(functools.partial(step_kernel, dims), out_shape=(rows, row...  66.7 us
    pallas_call x1, Pallas kernels, finish(): pl.pallas_call(functools.partial(finish_kernel, grad_scale), out_shape=(t...  2.04 us

profile of v3, /device:TPU:1, one launch (start us, length us, event | category | flops | bytes accessed | tf_op | source)
XLA Modules:
  0.0 69.4 jit_solution(10789223590476578973)
XLA Ops:
  0.6 66.7 %whole_step.1 = (bf16[8,64,128]{2,1,0:T(8,128)(2,1)}, bf16[8,64,128]{2,1,0:T(8,128)(2,1)}, bf16[8,64,128]{2,1,0:T(8,128)(2,1)}, bf16[512,128]{1,0:T(8,128)(2,1)}) custom-call(bf16[64,8,128]{2,1,0:T(8,128)(2,1)} %bitcast.14, bf16[64,8,128]{2,1,0:T(8,128)(2,1)} %bitcast.15, bf16[64,8,128]{2,1,0:T(8,128)(2,1)} %bitcast.16, f32[49,64]{1,0:T(8,128)} %bitcast.18, ...), custom_call_target="tpu_custom_call" | custom-call | tf_op jit(solution)/shard_map/whole_step/pallas_call | solution.py:1025
  67.3 2.0 %finish.1 = (bf16[64,8,128]{2,1,0:T(8,128)(2,1)}, bf16[64,8,128]{2,1,0:T(8,128)(2,1)}, bf16[64,8,128]{2,1,0:T(8,128)(2,1)}, f32[49,64]{1,0:T(8,128)}, f32[64,256...) custom-call(bf16[8,64,128]{2,1,0:T(8,128)(2,1)} %get-tuple-element.20.next_rows, ...), custom_call_target="tpu_custom_call" | custom-call | tf_op jit(solution)/shard_map/finish/pallas_call | solution.py:1054

commit v4 on v3

--- a/solution.py
+++ b/solution.py
@@ -124,6 +124,11 @@
         self.right = self.c == self.nc - 1
         self.row_edge = jnp.logical_or(self.top, self.bottom)
         self.col_edge = jnp.logical_or(self.left, self.right)
+        self.nx = self.nc // 2
+        self.core = self.r % 2
+        self.x = self.c % self.nx
+        self.near = self.x * 2 + self.core
+        self.z = (self.r // 2) * 2 + self.c // self.nx
         self.row_kind = jnp.where(self.top, 0, 1)
         self.col_kind = jnp.where(self.left, 0, 1)
 
@@ -153,11 +158,25 @@
         ]
 
     def ring(self, axis):
-        index, count = {"face": (self.f, self.nf), "row": (self.r, self.nr), "col": (self.c, self.nc)}[axis]
+        index, count = {
+            "face": (self.f, self.nf),
+            "near": (self.near, self.nx * 2),
+            "z": (self.z, self.nr),
+        }[axis]
         out = []
         for step in range(1, count):
             other = lax.rem(index + step, count)
-            out.append((other, self.at(**{axis[0]: other}), step))
+            if axis == "face":
+                device = self.at(f=other)
+            elif axis == "near":
+                device = self.at(
+                    r=self.r - self.core + other % 2, c=self.c - self.x + other // 2
+                )
+            else:
+                device = self.at(
+                    r=(other // 2) * 2 + self.core, c=(other % 2) * self.nx + self.x
+                )
+            out.append((other, device, step))
         return out
 
 
@@ -259,9 +278,6 @@
     cot,
     total,
     edge_grad,
-    ge,
-    gr,
-    gg,
     gc,
     grads,
     rim,
@@ -281,8 +297,6 @@
     a3,
     a4_src,
     a4,
-    a5_src,
-    a5,
     near,
     near_late,
     group_sem,
@@ -296,7 +310,6 @@
     s2,
     s3,
     s4,
-    s5,
 ):
     held = (x_ref, prior_ref, cot_ref, kernel_ref, we_ref, wr_ref, wg_ref, wc_ref, sf, sc)
     given = (x_in, prior_in, cot_in, kernel_in, we_in, wr_in, wg_in, wc_in, sf_in, sc_in)
@@ -310,24 +323,17 @@
         ref[...] = jnp.zeros_like(ref)
     at = Place(dims)
     nf, nr, nc = dims
-    part1 = PACK_ROWS // nf
-    part2 = part1 // nc
+    near_count = at.nx * 2
+    part1 = PACK_ROWS // near_count
     face_ring = at.ring("face")
-    row_ring = at.ring("row")
-    col_ring = at.ring("col")
+    near_ring = at.ring("near")
+    z_ring = at.ring("z")
     row_group = at.row_group()
     col_group = at.col_group()
     barrier = pltpu.get_barrier_semaphore()
-    for ring in (face_ring, row_ring, col_ring):
+    for ring in (face_ring, near_ring, z_ring):
         for unused, device, unused2 in ring:
             greet(barrier, device)
-    corner = at.at(r=nr - 1 - at.r, c=nc - 1 - at.c)
-    any_edge = jnp.logical_or(at.row_edge, at.col_edge)
-
-    @pl.when(any_edge)
-    def _():
-        greet(barrier, corner)
-
     above = at.at(r=jnp.maximum(at.r - 1, 0))
     below = at.at(r=jnp.minimum(at.r + 1, nr - 1))
     before = at.at(c=jnp.maximum(at.c - 1, 0))
@@ -336,52 +342,65 @@
     has_below = jnp.logical_not(at.bottom)
     has_before = jnp.logical_not(at.left)
     has_after = jnp.logical_not(at.right)
-
-    for row in range(PR):
-        spread[:, row * TC : (row + 1) * TC] = spread_block(row)
-    for ref in (ge, gr, gg, gc):
-        ref[...] = jnp.zeros_like(ref)
-    flip = flip_matrix()
-    edge_rows = jnp.zeros((RIM, CH, TC), BF)
-
-    @pl.when(at.top)
-    def _():
-        xw[0:RIM] = edge_rows
-
-    @pl.when(at.bottom)
-    def _():
-        xw[RIM + TR : PR] = edge_rows
-
-    for load in loads:
-        load.wait()
+    any_edge = jnp.logical_or(at.row_edge, at.col_edge)
+    expected = nf + near_count + nr - 3
+    for present, device in ((has_above, above), (has_below, below), (has_before, before), (has_after, after)):
+        expected = expected + jnp.where(present, 1, 0)
+
+        @pl.when(present)
+        def _(device=device):
+            greet(barrier, device)
+
+    @pl.when(any_edge)
+    def _():
+        for device, unused, unused2 in row_group:
+            greet(barrier, device)
+
+    loads[0].wait()
     natural[...] = x_ref[...].astype(F32).reshape(CH * TR, TC)
     for y in range(TR):
         xw[RIM + y] = natural[pl.ds(y, CH, stride=TR), :].astype(BF)
+    pl.semaphore_wait(barrier, expected + jnp.where(any_edge, 3, 0))
+
+    def to_above():
+        return send(xw.at[pl.ds(RIM, RIM)], xw.at[pl.ds(RIM + TR, RIM)], near.at[0, 0], near.at[1, 0], above)
+
+    def to_below():
+        return send(xw.at[pl.ds(TR, RIM)], xw.at[pl.ds(0, RIM)], near.at[0, 1], near.at[1, 1], below)
+
+    def own_edge():
+        return xw.at[pl.ds(jnp.where(at.top, RIM, TR), RIM)]
+
+    @pl.when(at.row_edge)
+    def _():
+        start_group(row_group, own_edge(), strips, group_sem, 0)
+
+    @pl.when(has_above)
+    def _():
+        to_above().start()
+
+    @pl.when(has_below)
+    def _():
+        to_below().start()
+
+    edge_rows = jnp.zeros((RIM, CH, TC), BF)
+
+    @pl.when(at.top)
+    def _():
+        xw[0:RIM] = edge_rows
+
+    @pl.when(at.bottom)
+    def _():
+        xw[RIM + TR : PR] = edge_rows
+
+    for row in range(PR):
+        spread[:, row * TC : (row + 1) * TC] = spread_block(row)
+    flip = flip_matrix()
+    for load in loads[1:]:
+        load.wait()
     prior[...] = prior_ref[...].astype(F32).reshape(CH * TR, TC)
     cot[...] = cot_ref[...].astype(F32).reshape(CH * TR, TC)
-    pl.semaphore_wait(barrier, nf + nr + nc - 3 + jnp.where(any_edge, 1, 0))
-
-    def to_above():
-        return send(xw.at[pl.ds(RIM, RIM)], xw.at[pl.ds(RIM + TR, RIM)], near.at[0, 0], near.at[1, 0], above)
-
-    def to_below():
-        return send(xw.at[pl.ds(TR, RIM)], xw.at[pl.ds(0, RIM)], near.at[0, 1], near.at[1, 1], below)
-
-    def own_edge():
-        return xw.at[pl.ds(jnp.where(at.top, RIM, TR), RIM)]
-
-    @pl.when(at.row_edge)
-    def _():
-        start_group(row_group, own_edge(), strips, group_sem, 0)
-
-    @pl.when(has_above)
-    def _():
-        to_above().start()
-
-    @pl.when(has_below)
-    def _():
-        to_below().start()
-
+    gc[:, 0 : KS * KS] = kernel_ref[...].T
     is_corner = jnp.logical_and(at.row_edge, at.col_edge)
 
     @pl.when(has_below)
@@ -527,8 +546,6 @@
         ef[row] = ends[:, row * TC : (row + 1) * TC]
     lane = lax.broadcasted_iota(jnp.int32, (PR, 8, TC), 2)
     lane2 = lax.broadcasted_iota(jnp.int32, (8, TC), 1)
-    kernel_t = kernel_ref[...].T
-    gc[:, 0 : KS * KS] = kernel_t
 
     def forward(g, carry):
         part = pl.ds(pl.multiple_of(g * 8, 8), 8)
@@ -552,8 +569,6 @@
         return carry
 
     lax.fori_loop(0, CH // 8, forward, 0)
-    gc[...] = jnp.zeros_like(gc)
-
     we = we_ref[...]
     wr_t = wr_ref[...]
     wg = wg_ref[...]
@@ -563,88 +578,85 @@
     wg_t = wg.T
     wc = wc_t.T
 
-    def chunk(i, carry):
-        r0 = i * 2
-
-        def pair(load):
-            return jnp.concatenate([load(r0), load(r0 + 1)], axis=1)
-
-        s = pair(lambda y: summed[y])
-        center = s - jnp.mean(s, axis=0, keepdims=True)
-        scale = lax.rsqrt(jnp.mean(center * center, axis=0, keepdims=True) + 1e-06)
-        unit = center * scale
-        normed = unit.astype(BF)
-        hidden = dot(we_t, normed)
-        acts = []
-        slopes = []
-        for start in range(0, HID, 32):
-            h = hidden[start : start + 32]
-            cdf = 0.5 + 0.5 * lax.erf(h * math.sqrt(0.5))
-            acts.append((h * cdf).astype(BF))
-            slopes.append(cdf + h * (jnp.exp(-0.5 * h * h) * (1.0 / math.sqrt(2.0 * math.pi))))
-        act = jnp.concatenate(acts, axis=0)
-        slope = jnp.concatenate(slopes, axis=0)
-        out = (pair(lambda y: xf[RIM + y]) + dot(wr_t, act)).astype(BF)
-        earlier = pair(lambda y: prior[pl.ds(y, CH, stride=TR), :])
-        joined = jnp.concatenate([out, earlier.astype(BF)], axis=0)
-        gates = jax.nn.sigmoid(dot(wg_t, joined))
-        update = gates[:CH]
-        reset = gates[CH:]
-        joined_reset = jnp.concatenate([out, (reset * earlier).astype(BF)], axis=0)
-        proposal = jnp.tanh(dot(wc_t, joined_reset))
-        result = (1.0 - update) * earlier + update * proposal
-        g = pair(lambda y: cot[pl.ds(y, CH, stride=TR), :])
-        d_cand = (g * update * (1.0 - proposal * proposal)).astype(BF)
-        d_joined_reset = dot(wc, d_cand)
-        d_reset = d_joined_reset[CH:]
-        d_gates = jnp.concatenate(
-            [
-                g * (proposal - earlier) * (update * (1.0 - update)),
-                d_reset * earlier * (reset * (1.0 - reset)),
-            ],
-            axis=0,
-        ).astype(BF)
-        d_joined = dot(wg, d_gates)
-        d_out = (d_joined_reset[:CH] + d_joined[:CH]).astype(BF)
-        d_prior = g * (1.0 - update) + d_reset * reset + d_joined[CH:]
-        d_hidden = (dot(wr, d_out) * slope).astype(BF)
-        d_normed = dot(we, d_hidden)
-        ge[...] += dot_nt(normed, d_hidden)
-        gr[...] += dot_nt(d_out, act)
-        gg[...] += dot_nt(joined, d_gates)
-        gc[...] += dot_nt(d_cand, joined_reset)
-        d_summed = scale * (
-            d_normed
-            - jnp.mean(d_normed, axis=0, keepdims=True)
-            - unit * jnp.mean(d_normed * unit, axis=0, keepdims=True)
-        )
-        d_center = d_out.astype(F32)
-        for j in range(2):
-            y = r0 + j
-            cut = slice(j * TC, (j + 1) * TC)
-            back[y] = d_summed[:, cut]
-            total[RIM + y] = d_center[:, cut]
-            next_out[y] = result[:, cut].astype(BF)
-            prior_out[y] = d_prior[:, cut].astype(BF)
-        return carry
-
-    lax.fori_loop(0, TR // 2, chunk, 0)
-    grads[0:64] = ge[:, :TC].astype(BF)
-    grads[64:128] = ge[:, TC:].astype(BF)
-    grads[128:192] = gr[:, :TC].astype(BF)
-    grads[192:256] = gr[:, TC:].astype(BF)
-    grads[256:384] = gg[...].astype(BF)
-    grads[384:448] = gc[...].astype(BF)
+    def cells(load):
+        return jnp.concatenate([load(y) for y in range(TR)], axis=1)
+
+    s = cells(lambda y: summed[y])
+    center = s - jnp.mean(s, axis=0, keepdims=True)
+    scale = lax.rsqrt(jnp.mean(center * center, axis=0, keepdims=True) + 1e-06)
+    unit = center * scale
+    normed = unit.astype(BF)
+    hidden = dot(we_t, normed)
+    acts = []
+    slopes = []
+    for start in range(0, HID, 32):
+        h = hidden[start : start + 32]
+        cdf = 0.5 + 0.5 * lax.erf(h * math.sqrt(0.5))
+        acts.append((h * cdf).astype(BF))
+        slopes.append(cdf + h * (jnp.exp(-0.5 * h * h) * (1.0 / math.sqrt(2.0 * math.pi))))
+    act = jnp.concatenate(acts, axis=0)
+    slope = jnp.concatenate(slopes, axis=0)
+    out = (cells(lambda y: xf[RIM + y]) + dot(wr_t, act)).astype(BF)
+    earlier = cells(lambda y: prior[pl.ds(y, CH, stride=TR), :])
+    joined = jnp.concatenate([out, earlier.astype(BF)], axis=0)
+    gates = jax.nn.sigmoid(dot(wg_t, joined))
+    update = gates[:CH]
+    reset = gates[CH:]
+    joined_reset = jnp.concatenate([out, (reset * earlier).astype(BF)], axis=0)
+    proposal = jnp.tanh(dot(wc_t, joined_reset))
+    result = (1.0 - update) * earlier + update * proposal
+    g = cells(lambda y: cot[pl.ds(y, CH, stride=TR), :])
+    d_cand = (g * update * (1.0 - proposal * proposal)).astype(BF)
+    d_joined_reset = dot(wc, d_cand)
+    d_reset = d_joined_reset[CH:]
+    d_gates = jnp.concatenate(
+        [
+            g * (proposal - earlier) * (update * (1.0 - update)),
+            d_reset * earlier * (reset * (1.0 - reset)),
+        ],
+        axis=0,
+    ).astype(BF)
+    d_joined = dot(wg, d_gates)
+    d_out = (d_joined_reset[:CH] + d_joined[:CH]).astype(BF)
+    d_prior = g * (1.0 - update) + d_reset * reset + d_joined[CH:]
+    d_hidden = (dot(wr, d_out) * slope).astype(BF)
+    d_normed = dot(we, d_hidden)
+    d_expand = dot_nt(normed, d_hidden).astype(BF)
+    d_reduce = dot_nt(d_out, act).astype(BF)
+    grads[0:64] = d_expand[:, :TC]
+    grads[64:128] = d_expand[:, TC:]
+    grads[128:192] = d_reduce[:, :TC]
+    grads[192:256] = d_reduce[:, TC:]
+    grads[256:384] = dot_nt(joined, d_gates).astype(BF)
+    grads[384:448] = dot_nt(d_cand, joined_reset).astype(BF)
+    d_summed = scale * (
+        d_normed
+        - jnp.mean(d_normed, axis=0, keepdims=True)
+        - unit * jnp.mean(d_normed * unit, axis=0, keepdims=True)
+    )
+    d_center = d_out.astype(F32)
+    for y in range(TR):
+        cut = slice(y * TC, (y + 1) * TC)
+        back[y] = d_summed[:, cut]
+        total[RIM + y] = d_center[:, cut]
+        next_out[y] = result[:, cut].astype(BF)
+        prior_out[y] = d_prior[:, cut].astype(BF)
 
     def piece1(other):
         return grads.at[pl.ds(pl.multiple_of(other * part1, part1), part1)]
 
     def start_shares(wanted):
-        for other, device, step in face_ring:
-
-            @pl.when((other == nf - 1) == wanted)
+        for other, device, step in near_ring:
+
+            @pl.when((other == near_count - 1) == wanted)
             def _(other=other, device=device, step=step):
-                send(piece1(other), a1.at[at.f], s1.at[0, step], s1.at[1, at.f], device).start()
+                send(piece1(other), a1.at[at.near], s1.at[0, step], s1.at[1, at.near], device).start()
+
+    def summed_slots(slots, count):
+        partial = slots[0].astype(F32)
+        for other in range(1, count):
+            partial = partial + slots[other].astype(F32)
+        return partial.astype(BF)
 
     start_shares(False)
 
@@ -662,7 +674,7 @@
     lax.fori_loop(0, CH // 8, backward_kernel, 0)
     grads[448:512] = gc[...].astype(BF)
     start_shares(True)
-    a1[at.f] = piece1(at.f)[...]
+    a1[at.near] = piece1(at.near)[...]
 
     def backward(g, carry):
         part = pl.ds(pl.multiple_of(g * 8, 8), 8)
@@ -712,17 +724,11 @@
     def _():
         rim_after().start()
 
-    wait_ring(face_ring, piece1, a1, s1)
-    partial = a1[0].astype(F32)
-    for other in range(1, nf):
-        partial = partial + a1[other].astype(F32)
+    wait_ring(near_ring, piece1, a1, s1)
+    partial = summed_slots(a1, near_count)
     a2_src[...] = partial
-
-    def piece2(other):
-        return a2_src.at[pl.ds(pl.multiple_of(other * part2, part2), part2)]
-
-    start_ring(col_ring, at.c, piece2, a2, s2)
-    a2[at.c] = piece2(at.c)[...]
+    start_ring(face_ring, at.f, lambda other: a2_src, a2, s2)
+    a2[at.f] = partial
 
     @pl.when(has_after)
     def _():
@@ -779,13 +785,11 @@
         start_group(row_group, corner_out, corner_strips, corner_group_sem, 0)
         corner_strips[at.row_kind * 2] = blocks.astype(BF)
 
-    wait_ring(col_ring, piece2, a2, s2)
-    partial = a2[0]
-    for other in range(1, nc):
-        partial = partial + a2[other]
+    wait_ring(face_ring, lambda other: a2_src, a2, s2)
+    partial = summed_slots(a2, nf)
     a3_src[...] = partial
-    start_ring(row_ring, at.r, lambda other: a3_src, a3, s3)
-    a3[at.r] = partial
+    start_ring(z_ring, at.z, lambda other: a3_src, a3, s3)
+    a3[at.z] = partial
 
     def seam_total(slots, kind, first_side):
         gathered = None
@@ -821,14 +825,6 @@
         edges[1] = total[RIM + TR : PR].astype(BF)
         grad_below().start()
 
-    wait_ring(row_ring, lambda other: a3_src, a3, s3)
-    partial = a3[0]
-    for other in range(1, nr):
-        partial = partial + a3[other]
-    a4_src[...] = partial
-    start_ring(col_ring, at.c, lambda other: a4_src, a4, s4)
-    a4[at.c] = partial
-
     @pl.when(at.row_edge)
     def _():
         row_faces[at.f] = own_grad()[...]
@@ -839,11 +835,11 @@
         start_group(row_group, row_chosen, row_strips, group_back, 2)
         row_strips[at.row_kind * 2] = strip
 
-    wait_ring(col_ring, lambda other: a4_src, a4, s4)
-    full = jnp.concatenate([a4[other] for other in range(nc)], axis=0).astype(BF)
-    a5_src[...] = full
-    start_ring(face_ring, at.f, lambda other: a5_src, a5, s5)
-    a5[at.f] = full
+    wait_ring(z_ring, lambda other: a3_src, a3, s3)
+    partial = summed_slots(a3, nr)
+    a4_src[...] = partial
+    start_ring(near_ring, at.near, lambda other: a4_src, a4, s4)
+    a4[at.near] = partial
 
     @pl.when(has_below)
     def _():
@@ -876,9 +872,9 @@
             total[first + i] = total[first + i] + dot(blocks.astype(BF), one_hot(wanted == lanes))
 
     input_out[...] = total[RIM : RIM + TR].astype(BF)
-    wait_ring(face_ring, lambda other: a5_src, a5, s5)
-    for other in range(nf):
-        grads_out[other * part1 : (other + 1) * part1] = a5[other]
+    wait_ring(near_ring, lambda other: a4_src, a4, s4)
+    for other in range(near_count):
+        grads_out[other * part1 : (other + 1) * part1] = a4[other]
 
     @pl.when(has_above)
     def _():
@@ -927,11 +923,10 @@
         done_ring(face_ring, lambda other: rim, rim_faces, rim_face_sem)
         done_group(col_group, rim_chosen, rim_strips, group_back, 0)
 
-    done_ring(face_ring, piece1, a1, s1)
-    done_ring(col_ring, piece2, a2, s2)
-    done_ring(row_ring, lambda other: a3_src, a3, s3)
-    done_ring(col_ring, lambda other: a4_src, a4, s4)
-    done_ring(face_ring, lambda other: a5_src, a5, s5)
+    done_ring(near_ring, piece1, a1, s1)
+    done_ring(face_ring, lambda other: a2_src, a2, s2)
+    done_ring(z_ring, lambda other: a3_src, a3, s3)
+    done_ring(near_ring, lambda other: a4_src, a4, s4)
 
 
 def finish_kernel(
@@ -970,8 +965,8 @@
 
 def whole_step(dims, *given):
     nf, nr, nc = dims
-    part1 = PACK_ROWS // nf
-    part2 = part1 // nc
+    near_count = nc // 2 * 2
+    part1 = PACK_ROWS // near_count
     wide = (PR, CH, TC)
     tile = (TR, CH, TC)
     strip = (RIM, CH, TC)
@@ -1002,10 +997,7 @@
         flat,
         wide,
         wide,
-        (CH, HID),
-        (CH, HID),
-        (2 * CH, 2 * CH),
-        (CH, 2 * CH),
+        (CH, TC),
     ]
     back_scratch = [
         (PACK_ROWS, TC),
@@ -1019,9 +1011,11 @@
         (nf,) + strip,
         strip,
         (4,) + strip,
-        (nf, part1, TC),
+        (near_count, part1, TC),
+        (part1, TC),
     ]
-    sum_scratch = [(part1, TC), (nc, part2, TC), (part2, TC), (nr, part2, TC), (part2, TC), (nc, part2, TC)]
+    share = (part1, TC)
+    sum_scratch = [(nf,) + share, share, (nr,) + share, share, (near_count,) + share]
     return pl.pallas_call(
         functools.partial(step_kernel, dims),
         out_shape=(rows, rows, rows, jax.ShapeDtypeStruct((PACK_ROWS, TC), BF)),
@@ -1036,11 +1030,10 @@
         + [pltpu.VMEM(shape, BF) for shape in bf16_scratch]
         + [pltpu.VMEM(shape, F32) for shape in f32_scratch]
         + [pltpu.VMEM(shape, BF) for shape in back_scratch]
-        + [pltpu.VMEM(shape, F32) for shape in sum_scratch]
-        + [pltpu.VMEM((part1, TC), BF), pltpu.VMEM((nf, part1, TC), BF)]
+        + [pltpu.VMEM(shape, BF) for shape in sum_scratch]
         + [dma(2, 4), dma(2, 2), dma(4, 4), dma(2, nf), dma(2, nf)]
         + [dma(2, 4), dma(4, 4), dma(2, nf), dma(2, nf)]
-        + [dma(2, nf), dma(2, nc), dma(2, nr), dma(2, nc), dma(2, nf)],
+        + [dma(2, near_count), dma(2, nf), dma(2, nr), dma(2, near_count)],
         compiler_params=pltpu.CompilerParams(
             collective_id=0, has_side_effects=True, vmem_limit_bytes=LIMIT
         ),

time: 70.6 us -> 64.1 us (0.908); the launches traced: 69.4 us -> 63.9 us
  Pallas kernels: 68.7 us -> 63.3 us
    pallas_call x1, Pallas kernels: 66.7 us -> 61.3 us  [whole_step(): pl.pallas_call(functools.partial(step_kernel, dims), out_shape=(rows, row...]
where the time goes in v4:
time: 64.1 us; the launch traced here: 63.9 us
  Pallas kernels  63.3 us (99%)
    pallas_call x1, Pallas kernels, whole_step(): pl.pallas_call(functools.partial(step_kernel, dims), out_shape=(rows, row...  61.3 us
    pallas_call x1, Pallas kernels, finish(): pl.pallas_call(functools.partial(finish_kernel, grad_scale), out_shape=(t...  2.04 us

profile of v4, /device:TPU:1, one launch (start us, length us, event | category | flops | bytes accessed | tf_op | source)
XLA Modules:
  0.0 63.9 jit_solution(7542504522667514177)
XLA Ops:
  0.6 61.3 %whole_step.1 = (bf16[8,64,128]{2,1,0:T(8,128)(2,1)}, bf16[8,64,128]{2,1,0:T(8,128)(2,1)}, bf16[8,64,128]{2,1,0:T(8,128)(2,1)}, bf16[512,128]{1,0:T(8,128)(2,1)}) custom-call(bf16[64,8,128]{2,1,0:T(8,128)(2,1)} %bitcast.14, bf16[64,8,128]{2,1,0:T(8,128)(2,1)} %bitcast.15, bf16[64,8,128]{2,1,0:T(8,128)(2,1)} %bitcast.16, f32[49,64]{1,0:T(8,128)} %bitcast.18, ...), custom_call_target="tpu_custom_call" | custom-call | tf_op jit(solution)/shard_map/whole_step/pallas_call | solution.py:1019
  61.9 2.0 %finish.1 = (bf16[64,8,128]{2,1,0:T(8,128)(2,1)}, bf16[64,8,128]{2,1,0:T(8,128)(2,1)}, bf16[64,8,128]{2,1,0:T(8,128)(2,1)}, f32[49,64]{1,0:T(8,128)}, f32[64,256...) custom-call(bf16[8,64,128]{2,1,0:T(8,128)(2,1)} %get-tuple-element.20.next_rows, ...), custom_call_target="tpu_custom_call" | custom-call | tf_op jit(solution)/shard_map/finish/pallas_call | solution.py:1047

commit v5 on v4

--- a/solution.py
+++ b/solution.py
@@ -17,6 +17,7 @@
 TC = 128
 PR = TR + 2 * RIM
 PACK_ROWS = 512
+LATE_ROW = 448
 BF = jnp.bfloat16
 F32 = jnp.float32
 MESH = pl.DeviceIdType.MESH
@@ -124,11 +125,9 @@
         self.right = self.c == self.nc - 1
         self.row_edge = jnp.logical_or(self.top, self.bottom)
         self.col_edge = jnp.logical_or(self.left, self.right)
-        self.nx = self.nc // 2
         self.core = self.r % 2
-        self.x = self.c % self.nx
-        self.near = self.x * 2 + self.core
-        self.z = (self.r // 2) * 2 + self.c // self.nx
+        self.near = self.c * 2 + self.core
+        self.z = self.r // 2
         self.row_kind = jnp.where(self.top, 0, 1)
         self.col_kind = jnp.where(self.left, 0, 1)
 
@@ -160,8 +159,8 @@
     def ring(self, axis):
         index, count = {
             "face": (self.f, self.nf),
-            "near": (self.near, self.nx * 2),
-            "z": (self.z, self.nr),
+            "near": (self.near, self.nc * 2),
+            "z": (self.z, self.nr // 2),
         }[axis]
         out = []
         for step in range(1, count):
@@ -169,13 +168,9 @@
             if axis == "face":
                 device = self.at(f=other)
             elif axis == "near":
-                device = self.at(
-                    r=self.r - self.core + other % 2, c=self.c - self.x + other // 2
-                )
+                device = self.at(r=self.r - self.core + other % 2, c=other // 2)
             else:
-                device = self.at(
-                    r=(other // 2) * 2 + self.core, c=(other % 2) * self.nx + self.x
-                )
+                device = self.at(r=other * 2 + self.core)
             out.append((other, device, step))
         return out
 
@@ -256,6 +251,9 @@
     corner_face_sem,
     corner_group_sem,
     pack_late,
+    late_pick,
+    turns,
+    picks,
     natural,
     xw,
     strips,
@@ -269,7 +267,7 @@
     spread,
     halo,
     xf,
-    ef,
+    met,
     shifted,
     taps,
     summed,
@@ -277,7 +275,7 @@
     prior,
     cot,
     total,
-    edge_grad,
+    edge_back,
     gc,
     grads,
     rim,
@@ -323,7 +321,8 @@
         ref[...] = jnp.zeros_like(ref)
     at = Place(dims)
     nf, nr, nc = dims
-    near_count = at.nx * 2
+    near_count = nc * 2
+    z_count = nr // 2
     part1 = PACK_ROWS // near_count
     face_ring = at.ring("face")
     near_ring = at.ring("near")
@@ -343,7 +342,7 @@
     has_before = jnp.logical_not(at.left)
     has_after = jnp.logical_not(at.right)
     any_edge = jnp.logical_or(at.row_edge, at.col_edge)
-    expected = nf + near_count + nr - 3
+    expected = nf + near_count + z_count - 3
     for present, device in ((has_above, above), (has_below, below), (has_before, before), (has_after, after)):
         expected = expected + jnp.where(present, 1, 0)
 
@@ -431,6 +430,39 @@
     @pl.when(has_after)
     def _():
         to_after().start()
+
+    lane = lax.broadcasted_iota(jnp.int32, (TR, 8, TC), 2)
+    lane2 = lax.broadcasted_iota(jnp.int32, (8, TC), 1)
+    xf[RIM : RIM + TR] = xw[RIM : RIM + TR].astype(F32)
+
+    def moved_rows(rows, d):
+        if d == 0:
+            return rows
+        inside = lane < TC - d if d > 0 else lane >= -d
+        return jnp.where(inside[: rows.shape[0]], pltpu.roll(rows, (-d) % TC, 2), 0.0)
+
+    def forward(g, carry):
+        part = pl.ds(pl.multiple_of(g * 8, 8), 8)
+        values = gc[part, :]
+        sums = [jnp.zeros((8, TC), F32)] * TR
+        own = xf[RIM : RIM + TR, part, :]
+        for b in range(KS):
+            rows = moved_rows(own, b - RIM)
+            shifted[b, RIM : RIM + TR, part, :] = rows
+            for a in range(KS):
+                tap = a * KS + b
+                weight = jnp.broadcast_to(values[:, tap : tap + 1], (8, TC))
+                taps[tap, part, :] = weight
+                low_y = max(0, RIM - a)
+                high_y = min(TR, TR + RIM - a)
+                product = weight[None] * rows[low_y + a - RIM : high_y + a - RIM]
+                for y in range(low_y, high_y):
+                    sums[y] = sums[y] + product[y - low_y]
+        for y in range(TR):
+            summed[y, part, :] = sums[y]
+        return carry
+
+    lax.fori_loop(0, CH // 8, forward, 0)
 
     @pl.when(at.row_edge)
     def _():
@@ -473,22 +505,43 @@
     def late_after():
         return send(pack_late, sides_late.at[0], near_late.at[0, 1], near_late.at[1, 1], after)
 
-    @pl.when(at.row_edge)
-    def _():
-        wait_ring(face_ring, lambda other: chosen, faces, row_face_sem)
-        strip = oriented(faces[sf[at.row_kind, at.f]].astype(F32), sc[at.row_kind, at.f], flip)
-        xw[pl.ds(jnp.where(at.top, 0, RIM + TR), RIM)] = strip
-        late = jnp.zeros((CH, TC), F32)
+    @pl.when(at.col_edge)
+    def _():
+        side = at.col_kind + 2
+        turns[0] = turn_matrix(sc[side, at.f])
+        turns[1] = turn_matrix(sc[side, partner_of(sf, side, at.f, nf)])
+
+    @pl.when(is_corner)
+    def _():
         source = lax.broadcasted_iota(jnp.int32, (TC, TC), 0)
         lanes = lax.broadcasted_iota(jnp.int32, (TC, TC), 1)
+        owner, block, row_turn, col_turn = corner_of(sf, sc, at.f, at.row_kind, at.col_kind)
+        turns[2] = one_hot(
+            corner_lanes(lanes, at.row_kind, at.col_kind, block, row_turn, col_turn) == source
+        )
+        for other in range(nf):
+            owner, block, row_turn, col_turn = corner_of(sf, sc, other, at.row_kind, at.col_kind)
+            wanted = corner_lanes(source, at.row_kind, at.col_kind, block, row_turn, col_turn)
+            picks[other * TC : (other + 1) * TC, :] = one_hot(jnp.where(owner == at.f, wanted, -1) == lanes)
+
+    @pl.when(at.row_edge)
+    def _():
+        code = sc[at.row_kind, at.f]
+        source = lax.broadcasted_iota(jnp.int32, (TC, TC), 0)
+        source = jnp.where(code >= 2, TC - 1 - source, source)
+        lanes = lax.broadcasted_iota(jnp.int32, (TC, TC), 1)
+        wanted = jnp.where(lanes % 8 < RIM, lanes % 8 + TC - RIM, lanes % 8 - RIM)
+        wanted = jnp.where(lanes % 8 < 2 * RIM, wanted, -1)
         first = jnp.where(at.top, 0, RIM + TR)
         for i in range(RIM):
-            wanted = jnp.where(lanes % 8 < RIM, lanes % 8 + TC - RIM, lanes % 8 - RIM)
-            wanted = jnp.where(
-                jnp.logical_and(lanes // 8 == first + i, lanes % 8 < 2 * RIM), wanted, -1
+            here = jnp.where(code % 2 == 1, RIM - 1 - i, i)
+            late_pick[i * TC : (i + 1) * TC, :] = one_hot(
+                jnp.where(lanes // 8 == first + here, wanted, -1) == source
             )
-            late = late + dot(strip[i], one_hot(wanted == source))
-        pack_late[...] = late.astype(BF)
+        wait_ring(face_ring, lambda other: chosen, faces, row_face_sem)
+        strip = faces[sf[at.row_kind, at.f]]
+        flat = jnp.concatenate([strip[i] for i in range(RIM)], axis=1)
+        pack_late[...] = dot(flat, late_pick[...]).astype(BF)
 
         @pl.when(has_before)
         def _():
@@ -498,23 +551,20 @@
         def _():
             late_after().start()
 
-    xf[...] = xw[...].astype(F32)
+        xw[pl.ds(jnp.where(at.top, 0, RIM + TR), RIM)] = oriented(strip.astype(F32), code, flip)
 
     @pl.when(at.col_edge)
     def _():
         side = at.col_kind + 2
         wait_ring(face_ring, lambda other: col_chosen, col_faces, col_face_sem)
         strip = col_faces[sf[side, at.f]]
-        sides[at.col_kind] = dot(strip, turn_matrix(sc[side, at.f])).astype(BF)
+        sides[at.col_kind] = dot(strip, turns[0]).astype(BF)
 
     @pl.when(is_corner)
     def _():
         wait_ring(face_ring, lambda other: corner_pack, corner_faces, corner_face_sem)
-        source = lax.broadcasted_iota(jnp.int32, (TC, TC), 0)
-        lanes = lax.broadcasted_iota(jnp.int32, (TC, TC), 1)
-        owner, block, row_turn, col_turn = corner_of(sf, sc, at.f, at.row_kind, at.col_kind)
-        pick = one_hot(corner_lanes(lanes, at.row_kind, at.col_kind, block, row_turn, col_turn) == source)
-        sides_late[at.col_kind] = dot(corner_faces[owner], pick).astype(BF)
+        owner, unused, unused2, unused3 = corner_of(sf, sc, at.f, at.row_kind, at.col_kind)
+        sides_late[at.col_kind] = dot(corner_faces[owner], turns[2]).astype(BF)
 
     @pl.when(has_after)
     def _():
@@ -541,34 +591,53 @@
         + jnp.where(low, sides_late[0].astype(F32), sides_late[1].astype(F32))
     ).astype(BF)
 
-    ends = dot(halo[...], spread[...])
-    for row in range(PR):
-        ef[row] = ends[:, row * TC : (row + 1) * TC]
-    lane = lax.broadcasted_iota(jnp.int32, (PR, 8, TC), 2)
-    lane2 = lax.broadcasted_iota(jnp.int32, (8, TC), 1)
-
-    def forward(g, carry):
+    xf[0:RIM] = xw[0:RIM].astype(F32)
+    xf[RIM + TR : PR] = xw[RIM + TR : PR].astype(F32)
+
+    def forward_rows(g, carry):
         part = pl.ds(pl.multiple_of(g * 8, 8), 8)
-        values = gc[part, :]
-        sums = jnp.zeros((TR, 8, TC), F32)
-        inside = xf[:, part, :]
-        outside = ef[:, part, :]
+        sums = [summed[y, part, :] for y in range(TR)]
+        over = xf[0:RIM, part, :]
+        under = xf[RIM + TR : PR, part, :]
         for b in range(KS):
-            d = b - RIM
-            rows = inside
-            if d:
-                wrapped = lane < d if d > 0 else lane >= TC + d
-                rows = pltpu.roll(jnp.where(wrapped, outside, inside), (-d) % TC, 2)
-            shifted[b, :, part, :] = rows
-            for a in range(KS):
-                tap = a * KS + b
-                weight = jnp.broadcast_to(values[:, tap : tap + 1], (8, TC))
-                taps[tap, part, :] = weight
-                sums = sums + weight[None] * rows[a : a + TR]
-        summed[:, part, :] = sums
+            rows_over = moved_rows(over, b - RIM)
+            rows_under = moved_rows(under, b - RIM)
+            shifted[b, 0:RIM, part, :] = rows_over
+            shifted[b, RIM + TR : PR, part, :] = rows_under
+            for y in range(TR):
+                for a in range(KS):
+                    if y + a < RIM:
+                        sums[y] = sums[y] + taps[a * KS + b, part, :] * rows_over[y + a]
+                    elif y + a >= RIM + TR:
+                        sums[y] = sums[y] + taps[a * KS + b, part, :] * rows_under[y + a - RIM - TR]
+        for y in range(TR):
+            summed[y, part, :] = sums[y]
         return carry
 
-    lax.fori_loop(0, CH // 8, forward, 0)
+    lax.fori_loop(0, CH // 8, forward_rows, 0)
+
+    def meets(b):
+        if b < RIM:
+            return jnp.logical_and(place >= b, place < RIM)
+        return jnp.logical_and(place >= RIM, place < b)
+
+    def exact_dot(product, values, other):
+        high = values.astype(BF)
+        return product(high, other) + product((values - high.astype(F32)).astype(BF), other)
+
+    padding = halo[...].astype(F32)
+    edge_cells = jnp.zeros((CH, TC), F32)
+    for b in range(KS):
+        if b == RIM:
+            continue
+        used = jnp.where(meets(b), padding, 0.0)
+        for a in range(KS):
+            tap = a * KS + b
+            rolled = pltpu.roll(used, (RIM - a * 8 - b) % TC, 1)
+            met[tap] = rolled
+            edge_cells = edge_cells + taps[tap] * rolled
+    ends = exact_dot(dot, edge_cells, spread[:, : TR * TC])
+
     we = we_ref[...]
     wr_t = wr_ref[...]
     wg = wg_ref[...]
@@ -581,7 +650,7 @@
     def cells(load):
         return jnp.concatenate([load(y) for y in range(TR)], axis=1)
 
-    s = cells(lambda y: summed[y])
+    s = cells(lambda y: summed[y]) + ends
     center = s - jnp.mean(s, axis=0, keepdims=True)
     scale = lax.rsqrt(jnp.mean(center * center, axis=0, keepdims=True) + 1e-06)
     unit = center * scale
@@ -635,6 +704,8 @@
         - unit * jnp.mean(d_normed * unit, axis=0, keepdims=True)
     )
     d_center = d_out.astype(F32)
+    d_edge = exact_dot(dot_nt, d_summed, spread[:, : TR * TC])
+    edge_back[...] = d_edge
     for y in range(TR):
         cut = slice(y * TC, (y + 1) * TC)
         back[y] = d_summed[:, cut]
@@ -648,7 +719,7 @@
     def start_shares(wanted):
         for other, device, step in near_ring:
 
-            @pl.when((other == near_count - 1) == wanted)
+            @pl.when((other >= LATE_ROW // part1) == wanted)
             def _(other=other, device=device, step=step):
                 send(piece1(other), a1.at[at.near], s1.at[0, step], s1.at[1, at.near], device).start()
 
@@ -659,6 +730,34 @@
         return partial.astype(BF)
 
     start_shares(False)
+
+    d_padding = jnp.zeros((CH, TC), F32)
+    for b in range(KS):
+        if b == RIM:
+            continue
+        found = jnp.zeros((CH, TC), F32)
+        for a in range(KS):
+            found = found + taps[a * KS + b] * pltpu.roll(d_edge, (a * 8 + b - RIM) % TC, 1)
+        d_padding = d_padding + jnp.where(meets(b), found, 0.0)
+    rim[...] = d_padding.astype(BF)
+
+    def rim_before():
+        return send(rim, rim_sides.at[1], near_back.at[0, 2], near_back.at[1, 2], before)
+
+    def rim_after():
+        return send(rim, rim_sides.at[0], near_back.at[0, 3], near_back.at[1, 3], after)
+
+    @pl.when(has_before)
+    def _():
+        rim_before().start()
+
+    @pl.when(has_after)
+    def _():
+        rim_after().start()
+
+    @pl.when(at.col_edge)
+    def _():
+        start_ring(face_ring, at.f, lambda other: rim, rim_faces, rim_face_sem)
 
     def backward_kernel(g, carry):
         part = pl.ds(pl.multiple_of(g * 8, 8), 8)
@@ -667,6 +766,8 @@
         for b in range(KS):
             for a in range(KS):
                 terms = jnp.sum(rows * shifted[b, a : a + TR, part, :], axis=0)
+                if b != RIM:
+                    terms = terms + edge_back[part, :] * met[a * KS + b, part, :]
                 found = jnp.where(lane2 == a * KS + b, jnp.sum(terms, axis=1, keepdims=True), found)
         gc[part, :] = found
         return carry
@@ -676,11 +777,12 @@
     start_shares(True)
     a1[at.near] = piece1(at.near)[...]
 
+    lane_all = lax.broadcasted_iota(jnp.int32, (PR, 8, TC), 2)
+
     def backward(g, carry):
         part = pl.ds(pl.multiple_of(g * 8, 8), 8)
         rows = back[:, part, :]
         inner = jnp.zeros((PR, 8, TC), F32)
-        outer = jnp.zeros((PR, 8, TC), F32)
         for b in range(KS):
             d = b - RIM
             columns = [None] * PR
@@ -689,47 +791,16 @@
                 for y in range(TR):
                     columns[y + a] = product[y] if columns[y + a] is None else columns[y + a] + product[y]
             moved = jnp.stack(columns)
-            if d == 0:
-                inner = inner + moved
-                continue
-            moved = pltpu.roll(moved, d % TC, 2)
-            wrapped = lane < d if d > 0 else lane >= TC + d
-            inner = inner + jnp.where(wrapped, 0.0, moved)
-            outer = outer + jnp.where(wrapped, moved, 0.0)
+            if d:
+                inside = lane_all < TC + d if d < 0 else lane_all >= d
+                moved = jnp.where(inside, pltpu.roll(moved, d % TC, 2), 0.0)
+            inner = inner + moved
         total[0:RIM, part, :] = inner[0:RIM]
         total[RIM : RIM + TR, part, :] = total[RIM : RIM + TR, part, :] + inner[RIM : RIM + TR]
         total[RIM + TR :, part, :] = inner[RIM + TR :]
-        edge_grad[:, part, :] = outer
         return carry
 
     lax.fori_loop(0, CH // 8, backward, 0)
-    flat = jnp.concatenate([edge_grad[row] for row in range(PR)], axis=1).astype(BF)
-    rim[...] = dot_nt(flat, spread[...]).astype(BF)
-
-    def rim_before():
-        return send(rim, rim_sides.at[1], near_back.at[0, 2], near_back.at[1, 2], before)
-
-    def rim_after():
-        return send(rim, rim_sides.at[0], near_back.at[0, 3], near_back.at[1, 3], after)
-
-    @pl.when(at.col_edge)
-    def _():
-        start_ring(face_ring, at.f, lambda other: rim, rim_faces, rim_face_sem)
-
-    @pl.when(has_before)
-    def _():
-        rim_before().start()
-
-    @pl.when(has_after)
-    def _():
-        rim_after().start()
-
-    wait_ring(near_ring, piece1, a1, s1)
-    partial = summed_slots(a1, near_count)
-    a2_src[...] = partial
-    start_ring(face_ring, at.f, lambda other: a2_src, a2, s2)
-    a2[at.f] = partial
-
     @pl.when(has_after)
     def _():
         rim_before().wait_recv()
@@ -752,6 +823,12 @@
     def _():
         edges[at.row_kind] = total[pl.ds(jnp.where(at.top, 0, RIM + TR), RIM)].astype(BF)
         start_ring(face_ring, at.f, lambda other: own_grad(), row_faces, row_back_sem)
+
+    wait_ring(near_ring, piece1, a1, s1)
+    partial = summed_slots(a1, near_count)
+    a2_src[...] = partial
+    start_ring(z_ring, at.z, lambda other: a2_src, a2, s2)
+    a2[at.z] = partial
 
     @pl.when(at.col_edge)
     def _():
@@ -766,30 +843,24 @@
         )
         keep = jnp.logical_and(low == at.left, jnp.logical_not(beyond))
         strip = jnp.where(keep, strip, 0.0).astype(BF)
-        turned = dot(strip, turn_matrix(sc[side, taker])).astype(BF)
+        turned = dot(strip, turns[1]).astype(BF)
         rim_chosen[...] = turned
         start_group(col_group, rim_chosen, rim_strips, group_back, 0)
         rim_strips[at.col_kind * 2] = turned
 
     @pl.when(is_corner)
     def _():
-        source = lax.broadcasted_iota(jnp.int32, (TC, TC), 0)
-        lanes = lax.broadcasted_iota(jnp.int32, (TC, TC), 1)
-        blocks = jnp.zeros((CH, TC), F32)
-        for other in range(nf):
-            owner, block, row_turn, col_turn = corner_of(sf, sc, other, at.row_kind, at.col_kind)
-            wanted = corner_lanes(source, at.row_kind, at.col_kind, block, row_turn, col_turn)
-            wanted = jnp.where(owner == at.f, wanted, -1)
-            blocks = blocks + dot(rim_faces[other], one_hot(wanted == lanes))
+        packs = jnp.concatenate([rim_faces[other] for other in range(nf)], axis=1)
+        blocks = dot(packs, picks[...])
         corner_out[...] = blocks.astype(BF)
         start_group(row_group, corner_out, corner_strips, corner_group_sem, 0)
         corner_strips[at.row_kind * 2] = blocks.astype(BF)
 
-    wait_ring(face_ring, lambda other: a2_src, a2, s2)
-    partial = summed_slots(a2, nf)
+    wait_ring(z_ring, lambda other: a2_src, a2, s2)
+    partial = summed_slots(a2, z_count)
     a3_src[...] = partial
-    start_ring(z_ring, at.z, lambda other: a3_src, a3, s3)
-    a3[at.z] = partial
+    start_ring(face_ring, at.f, lambda other: a3_src, a3, s3)
+    a3[at.f] = partial
 
     def seam_total(slots, kind, first_side):
         gathered = None
@@ -835,8 +906,8 @@
         start_group(row_group, row_chosen, row_strips, group_back, 2)
         row_strips[at.row_kind * 2] = strip
 
-    wait_ring(z_ring, lambda other: a3_src, a3, s3)
-    partial = summed_slots(a3, nr)
+    wait_ring(face_ring, lambda other: a3_src, a3, s3)
+    partial = summed_slots(a3, nf)
     a4_src[...] = partial
     start_ring(near_ring, at.near, lambda other: a4_src, a4, s4)
     a4[at.near] = partial
@@ -924,8 +995,8 @@
         done_group(col_group, rim_chosen, rim_strips, group_back, 0)
 
     done_ring(near_ring, piece1, a1, s1)
-    done_ring(face_ring, lambda other: a2_src, a2, s2)
-    done_ring(z_ring, lambda other: a3_src, a3, s3)
+    done_ring(z_ring, lambda other: a2_src, a2, s2)
+    done_ring(face_ring, lambda other: a3_src, a3, s3)
     done_ring(near_ring, lambda other: a4_src, a4, s4)
 
 
@@ -965,7 +1036,8 @@
 
 def whole_step(dims, *given):
     nf, nr, nc = dims
-    near_count = nc // 2 * 2
+    near_count = nc * 2
+    z_count = nr // 2
     part1 = PACK_ROWS // near_count
     wide = (PR, CH, TC)
     tile = (TR, CH, TC)
@@ -988,7 +1060,7 @@
     ]
     f32_scratch = [
         wide,
-        wide,
+        (KS * KS, CH, TC),
         (KS,) + wide,
         (KS * KS, CH, TC),
         tile,
@@ -996,8 +1068,8 @@
         flat,
         flat,
         wide,
-        wide,
-        (CH, TC),
+        edge,
+        edge,
     ]
     back_scratch = [
         (PACK_ROWS, TC),
@@ -1015,7 +1087,7 @@
         (part1, TC),
     ]
     share = (part1, TC)
-    sum_scratch = [(nf,) + share, share, (nr,) + share, share, (near_count,) + share]
+    sum_scratch = [(z_count,) + share, share, (nf,) + share, share, (near_count,) + share]
     return pl.pallas_call(
         functools.partial(step_kernel, dims),
         out_shape=(rows, rows, rows, jax.ShapeDtypeStruct((PACK_ROWS, TC), BF)),
@@ -1025,7 +1097,8 @@
         + [pltpu.SMEM(value.shape, value.dtype) for value in given[8:]]
         + [dma(10)]
         + [pltpu.VMEM((2,) + edge, BF), pltpu.VMEM(edge, BF), pltpu.VMEM((nf,) + edge, BF)]
-        + [pltpu.VMEM(edge, BF), pltpu.VMEM((4,) + edge, BF), dma(2, nf), dma(2, 4), pltpu.VMEM(edge, BF)]
+        + [pltpu.VMEM(edge, BF), pltpu.VMEM((4,) + edge, BF), dma(2, nf), dma(2, 4), pltpu.VMEM(edge, BF), pltpu.VMEM((RIM * TC, TC), BF)]
+        + [pltpu.VMEM((3, TC, TC), BF), pltpu.VMEM((nf * TC, TC), BF)]
         + [pltpu.VMEM(flat, F32)]
         + [pltpu.VMEM(shape, BF) for shape in bf16_scratch]
         + [pltpu.VMEM(shape, F32) for shape in f32_scratch]
@@ -1033,7 +1106,7 @@
         + [pltpu.VMEM(shape, BF) for shape in sum_scratch]
         + [dma(2, 4), dma(2, 2), dma(4, 4), dma(2, nf), dma(2, nf)]
         + [dma(2, 4), dma(4, 4), dma(2, nf), dma(2, nf)]
-        + [dma(2, near_count), dma(2, nf), dma(2, nr), dma(2, near_count)],
+        + [dma(2, near_count), dma(2, z_count), dma(2, nf), dma(2, near_count)],
         compiler_params=pltpu.CompilerParams(
             collective_id=0, has_side_effects=True, vmem_limit_bytes=LIMIT
         ),

time: 64.1 us -> 61.3 us (0.956)
  Pallas kernels: 63.3 us -> 60.5 us
    pallas_call x1, Pallas kernels: 61.3 us -> 58.5 us  [whole_step(): pl.pallas_call(functools.partial(step_kernel, dims), out_shape=(rows, row...]
where the time goes in v5:
time: 61.3 us; the launch traced here: 61.1 us
  Pallas kernels  60.5 us (99%)
  between operations  0.64 us (1%)
    pallas_call x1, Pallas kernels, whole_step(): pl.pallas_call(functools.partial(step_kernel, dims), out_shape=(rows, row...  58.5 us
    pallas_call x1, Pallas kernels, finish(): pl.pallas_call(functools.partial(finish_kernel, grad_scale), out_shape=(t...  2.04 us

profile of v5, /device:TPU:1, one launch (start us, length us, event | category | flops | bytes accessed | tf_op | source)
XLA Modules:
  0.0 61.1 jit_solution(12226634303625933096)
XLA Ops:
  0.6 58.5 %whole_step.1 = (bf16[8,64,128]{2,1,0:T(8,128)(2,1)}, bf16[8,64,128]{2,1,0:T(8,128)(2,1)}, bf16[8,64,128]{2,1,0:T(8,128)(2,1)}, bf16[512,128]{1,0:T(8,128)(2,1)}) custom-call(bf16[64,8,128]{2,1,0:T(8,128)(2,1)} %bitcast.14, bf16[64,8,128]{2,1,0:T(8,128)(2,1)} %bitcast.15, bf16[64,8,128]{2,1,0:T(8,128)(2,1)} %bitcast.16, f32[49,64]{1,0:T(8,128)} %bitcast.18, ...), custom_call_target="tpu_custom_call" | custom-call | tf_op jit(solution)/shard_map/whole_step/pallas_call | solution.py:1091
  59.1 2.0 %finish.1 = (bf16[64,8,128]{2,1,0:T(8,128)(2,1)}, bf16[64,8,128]{2,1,0:T(8,128)(2,1)}, bf16[64,8,128]{2,1,0:T(8,128)(2,1)}, f32[49,64]{1,0:T(8,128)}, f32[64,256...) custom-call(bf16[8,64,128]{2,1,0:T(8,128)(2,1)} %get-tuple-element.20.next_rows, ...), custom_call_target="tpu_custom_call" | custom-call | tf_op jit(solution)/shard_map/finish/pallas_call | solution.py:1120
